TPU v7x, 256 devices: a whole 4x4x8 slice. The times are simulated.
256 devices in a mesh: ctx: 16 (over y, x_lo, core), chan: 16 (over x_hi, z).
Axes of the slice: x: 4 (x_hi: 2, x_lo: 2; x = x_hi * 2 + x_lo), y: 4, z: 8, core: 2. Of those that a mesh axis runs over, the one named last changes fastest.
Arguments:
- features: bfloat16 [3, 12288, 8192], P(None, 'ctx', 'chan'), may hold values from -6 to 6
- pool_tails: bfloat16 [32, 3, 133, 8192], P('ctx', None, None, 'chan'), may hold values from -6 to 6
- short_filter: bfloat16 [7, 3, 8192], P(None, None, 'chan'), may hold values from -2 to 2
- long_filter: bfloat16 [512, 128], P('chan'), may hold values from -0.5 to 0.5
- skip_gain: float32 [8192], P('chan'), may hold values from -4 to 4
- out_weight: bfloat16 [8192, 8192], P('chan', 'ctx'), may hold values from -0.09375 to 0.09375
- stripe_request: int32 [16], replicated, may hold values from 0 to 3, never falling along the last dimension, each value on 1 to 8 neighbouring positions
- hit_holder: int32 [4], replicated, may hold values from 0 to 15
- hit_block: int32 [4], replicated, may hold values from 0 to 1
Outputs:
- mixed: bfloat16 [12288, 8192], P('ctx', 'chan')
Inputs may be any that keep to these rules, and one draw needn't show every extreme that they name: `stripe_request`: request ids never fall along the stripes, and every request holds one or more stripes.
All inputs are finite; a program needn't handle non-finite values.
Results may differ from a plain program's by a relative error of at most 0.018.
Values may be sent and summed in bfloat16 or wider, within the bound.
No kernel may reach another device: no remote copies, remote signals or barrier semaphores. Data moves between devices by JAX's collectives and lax.ppermute only.
A program may use at most 128 MiB of HBM per device.

v0:
```python
import jax
import jax.numpy as jnp
from jax import lax
from jax.sharding import PartitionSpec as P


def passed_along(value, axis, steps):
    count = lax.axis_size(axis)
    leading, last = (max(0, -steps), min(count, count - steps))
    return lax.ppermute(value, axis, [(source, source + steps) for source in range(leading, last)])


def short_filtering(extended, taps):
    short_len = taps.shape[0]
    length = extended.shape[1] - short_len + 1
    total = jnp.zeros((extended.shape[0], length, extended.shape[2]), jnp.float32)
    for offset in range(short_len):
        begin = short_len - 1 - offset
        total = total + taps[offset][:, None, :] * extended[:, begin : begin + length, :].astype(
            jnp.float32
        )
    return total


def toeplitz_long(product, filters, tokens):
    groups = filters.shape[0]
    long_len = filters.shape[1]
    channels = product.shape[1]
    padded = jnp.concatenate([jnp.zeros((1, channels), jnp.bfloat16), product], axis=0)
    block_count = tokens // long_len
    first = padded[:tokens].reshape(block_count, long_len, channels)
    second = padded[long_len : long_len + tokens].reshape(block_count, long_len, channels)
    windows = jnp.concatenate([first, second], axis=1).reshape(
        block_count, 2 * long_len, groups, channels // groups
    )
    out_rows = jnp.arange(long_len, dtype=jnp.int32)[:, None]
    in_rows = jnp.arange(2 * long_len, dtype=jnp.int32)[None, :]
    lagged = long_len + out_rows - in_rows
    valid = jnp.logical_and(lagged >= 0, lagged < long_len)
    picked = jnp.take(filters, jnp.clip(lagged, 0, long_len - 1), axis=1)
    kernel = jnp.where(valid[None, :, :], picked, jnp.zeros_like(picked))
    result = jnp.einsum("gij,njgc->nigc", kernel, windows, preferred_element_type=jnp.float32)
    return result.reshape(tokens, channels)


def body(
    features,
    pool_tails,
    short_filter,
    long_filter,
    skip_gain,
    out_weight,
    stripe_request,
    hit_holder,
    hit_block,
):
    tokens = features.shape[1]
    tail = pool_tails.shape[2]
    pool_dev = pool_tails.shape[0]
    long_len = long_filter.shape[1]
    my_index = lax.axis_index("ctx")
    request = stripe_request[my_index]
    earlier = stripe_request[jnp.maximum(my_index - 1, 0)]
    starting = jnp.logical_or(my_index == 0, earlier != request)
    taps = short_filter.astype(jnp.float32)
    all_starts = jnp.concatenate(
        [jnp.ones((1,), jnp.bool_), stripe_request[1:] != stripe_request[:-1]]
    )
    holders = hit_holder[stripe_request]
    blocks = hit_block[stripe_request]
    wanted = jnp.logical_and(all_starts, holders == my_index)
    select = jnp.logical_and(
        blocks[:, None] == jnp.arange(pool_dev, dtype=jnp.int32)[None, :], wanted[:, None]
    ).astype(jnp.bfloat16)
    slots = jnp.einsum(
        "dp,pstc->dstc", select, pool_tails, preferred_element_type=jnp.float32
    ).astype(jnp.bfloat16)
    arrived = lax.all_to_all(slots, "ctx", split_axis=0, concat_axis=0, tiled=True)
    pulled = jnp.sum(arrived.astype(jnp.float32), axis=0).astype(jnp.bfloat16)
    previous = passed_along(features[:, tokens - tail :, :], "ctx", 1)
    rim = jnp.where(starting, pulled, previous)
    filtered = short_filtering(jnp.concatenate([rim, features], axis=1), taps)
    product = (filtered[1] * filtered[2]).astype(jnp.bfloat16)
    query = filtered[0, long_len - 1 :]
    long_out = toeplitz_long(product, long_filter, tokens)
    direct = product[long_len - 1 :].astype(jnp.float32)
    gated = (query * (long_out + skip_gain[None, :] * direct)).astype(jnp.bfloat16)
    terms = jnp.dot(
        gated,
        lax.all_gather(out_weight, "ctx", axis=1, tiled=True),
        preferred_element_type=jnp.float32,
    )
    return lax.psum_scatter(terms.astype(jnp.bfloat16), "chan", scatter_dimension=1, tiled=True)


def solution(mesh):
    return jax.shard_map(
        body,
        mesh=mesh,
        in_specs=(
            P(None, "ctx", "chan"),
            P("ctx", None, None, "chan"),
            P(None, None, "chan"),
            P("chan", None),
            P("chan"),
            P("chan", "ctx"),
            P(),
            P(),
            P(),
        ),
        out_specs=P("ctx", "chan"),
        check_vma=False,
    )
```

profile of v0, /device:TPU:1, one launch (start us, length us, event | category | flops | bytes accessed | tf_op | source)
XLA Modules:
  0.0 464.1 jit_solution(14138916319929966136)
XLA Ops:
  6.5 0.0 copy-start
  6.5 0.0 all-gather.2.cloned.1.call-start
  6.5 0.7 all-gather.2.cloned.1.call-update
  7.3 0.7 compare_select_fusion.2
  7.9 1.3 gather_fusion.1
  9.2 1.3 gather_fusion
  10.6 0.8 slice_compare_fusion
  11.4 0.1 add_and_fusion
  11.5 0.0 copy-done
  11.5 2.5 convolution_convert_fusion.1
  14.0 6.5 %copy.19 = bf16[16,3,133,512]{3,2,1,0:T(8,128)(2,1)} copy(bf16[16,3,133,512]{3,0,2,1:T(8,128)(2,1)S(1)} %convolution_convert_fusion.1) | data formatting | bytes 13074432 | tf_op jit(solution)/shard_map/convert_element_type | solution.py:77
  20.4 7.7 %all-to-all-start = ((bf16[16,3,133,512]{3,2,1,0:T(8,128)(2,1)}), bf16[16,3,133,512]{3,2,1,0:T(8,128)(2,1)}, u32[]{:S(2)}, u32[]{:S(2)}) async-start(bf16[16,3,133,512]{3,2,1,0:T(8,128)(2,1)} %copy.19), calls=%async_computation | async-start | bytes 13369344 | tf_op jit(solution)/shard_map/all_to_all | solution.py:78
  28.1 0.0 copy-start.5
  28.1 0.0 copy-start.3
  28.1 0.0 reduce-scatter.2.cloned.1.call-start
  28.2 1.9 slice.71
  30.1 3.7 collective-permute-start
  33.8 2.8 copy.22
  36.7 0.0 copy-done.5
  36.7 0.1 copy.25
  36.8 0.0 copy-done.3
  36.9 0.1 fusion.28
  37.0 0.1 copy.38
  37.1 115.0 %gather_fusion.2 = bf16[32768,32]{1,0:T(8,128)(2,1)} fusion(bf16[32,128]{0,1:T(8,128)(2,1)S(1)} %copy.25, s32[32768]{0:T(1024)S(1)} %broadcast_clamp_fusion), kind=kCustom, calls=%fused_computation.2 | custom fusion | bytes 4325376 | tf_op jit(solution)/shard_map/jit(_take)/gather | solution.py:40
  152.0 0.0 copy-start.6
  152.0 8.6 %copy.26 = bf16[128,256,32]{1,0,2:T(8,128)(2,1)} copy(bf16[128,256,32]{2,1,0:T(8,128)(2,1)} %bitcast.67) | data formatting | bytes 4194304 | tf_op jit(solution)/shard_map/jit(_take)/gather | solution.py:40
  160.7 0.0 copy-done.6
  160.7 0.6 fusion.46
  162.5 0.2 fusion.33
  162.7 0.0 all-to-all-done
  162.7 4.0 reduce_sum.12
  166.8 0.0 collective-permute-done
  166.8 1.8 broadcast_select_fusion
  168.6 1.3 copy.21
  169.9 10.1 %multiply_add_fusion = f32[3,895,512]{1,2,0:T(8,128)S(1)} fusion(bf16[3,768,512]{1,2,0:T(8,128)(2,1)S(1)} %copy.22, bf16[3,133,512]{1,2,0:T(8,128)(2,1)S(1)} %copy.21, f32[3,512]{1,0:T(4,128)S(1)} %get-tuple-element.16, f32[3,512]{1,0:T(4,128)S(1)} %get-tuple-element.17, f32[3,512]{1,0:T(4,128)S(1)} %get-tuple-element.18, ...), kind=kLoop, calls=%fused_computation.10 | loop fusion | flops 56363520 | bytes 8309760 | tf_op jit(solution)/shard_map/add | solution.py:19
  180.0 0.0 copy-start.2
  180.0 2.5 copy-done.2
  182.5 0.2 fusion.12
  182.6 0.4 slice.118
  183.1 0.9 concatenate.25
  184.0 1.0 copy.24
  185.0 2.2 fusion.49
  187.2 0.5 pad_slice_fusion.12
  187.7 0.9 concatenate.24
  188.6 0.1 copy.23
  188.7 0.0 copy-start.4
  188.7 2.6 fusion.18
  191.4 1.9 copy.27
  193.3 0.0 all-gather.2.cloned.1.call-done
  193.3 0.0 copy-done.4
  193.3 14.2 %convolution_convert_fusion = bf16[768,8192]{1,0:T(8,128)(2,1)} fusion(bf16[512,8192]{1,0:T(8,128)(2,1)} %all-gather.2.cloned.1.call-done, f32[64,8,6,128]{3,2,1,0:T(8,128)} %bitcast.68, f32[3,895,512]{1,2,0:T(8,128)} %copy-done.2, f32[512]{0:T(512)S(1)} %copy-done.4, bf16[1,895,512]{1,2,0:T(8,128)(2,1)S(1)} %fusion.12), kind=kOutput, calls=%fused_computation.3 | convolution fusion | flops 6450708480 | bytes 25430016 | tf_op jit(solution)/shard_map/dot_general | solution.py:88
  207.5 0.0 copy-start.1
  207.5 0.0 reduce-scatter.2.cloned.1.call-update
  207.5 249.7 %reduce-scatter.2.cloned.1.call-done = bf16[768,512]{1,0:T(8,128)(2,1)} async-done(((bf16[768,8192]{1,0:T(8,128)(2,1)}), bf16[768,512]{1,0:T(8,128)(2,1)}) %reduce-scatter.2.cloned.1.call-update) | async-done | bytes 786448 | tf_op jit(solution)/shard_map/reduce_scatter | solution.py:93
  457.3 0.0 copy-done.1
  (8 shorter events, 0.1 us)
Async XLA Ops:
  6.5 4.9 %copy-start = (bf16[2,3,133,512]{3,0,2,1:T(2,128)(2,1)S(1)}, bf16[2,3,133,512]{3,0,2,1:T(2,128)(2,1)}, u32[]{:S(2)}) copy-start(bf16[2,3,133,512]{3,0,2,1:T(2,128)(2,1)} %param.10) | copy-start | bytes 2451460
  6.5 186.8 %all-gather.2.cloned.1.call-start = ((), (), s32[]{:S(2)}) async-start(), calls=%async_computation.2 | async-start | bytes 8912896 | tf_op jit(solution)/shard_map/all_gather | solution.py:90
  20.4 142.3 %all-to-all-start = ((bf16[16,3,133,512]{3,2,1,0:T(8,128)(2,1)}), bf16[16,3,133,512]{3,2,1,0:T(8,128)(2,1)}, u32[]{:S(2)}, u32[]{:S(2)}) async-start(bf16[16,3,133,512]{3,2,1,0:T(8,128)(2,1)} %copy.19), calls=%async_computation | async-start | bytes 13369344 | tf_op jit(solution)/shard_map/all_to_all | solution.py:78
  28.1 8.5 %copy-start.5 = (bf16[32,128]{1,0:T(8,128)(2,1)S(1)}, bf16[32,128]{1,0:T(8,128)(2,1)}, u32[]{:S(2)}) copy-start(bf16[32,128]{1,0:T(8,128)(2,1)} %param.12) | copy-start | bytes 24580
  28.1 8.7 %copy-start.3 = (bf16[7,3,512]{2,0,1:T(8,128)(2,1)S(1)}, bf16[7,3,512]{2,0,1:T(8,128)(2,1)}, u32[]{:S(2)}) copy-start(bf16[7,3,512]{2,0,1:T(8,128)(2,1)} %param.11) | copy-start | bytes 64516
  28.1 429.1 %reduce-scatter.2.cloned.1.call-start = ((), (), s32[]{:S(2)}) async-start(), calls=%async_computation.3 | async-start | bytes 13369344 | tf_op jit(solution)/shard_map/reduce_scatter | solution.py:93
  30.1 136.7 %collective-permute-start = (bf16[3,133,512]{2,1,0:T(8,128)(2,1)}, bf16[3,133,512]{2,1,0:T(8,128)(2,1)}, u32[]{:S(2)}, u32[]{:S(2)}) collective-permute-start(bf16[3,133,512]{2,1,0:T(8,128)(2,1)} %slice.71), channel_id=1, source_target_pairs={{0,16},{16,32},{32,48},{48,64},{64,80},{80,96},{96,112},{112,128},... | collective-permute-start | bytes 1225736 | tf_op jit(solution)/shard_map/ppermute | solution.py:10
  152.0 8.6 %copy-start.6 = (s32[16]{0:T(128)S(1)}, s32[16]{0:T(128)}, u32[]{:S(2)}) copy-start(s32[16]{0:T(128)} %param.15) | copy-start | bytes 196
  180.0 2.5 copy-start.2
  188.7 4.6 copy-start.4
  207.5 249.7 %copy-start.1 = (bf16[2,3,133,512]{3,0,2,1:T(2,128)(2,1)S(1)}, bf16[2,3,133,512]{3,0,2,1:T(2,128)(2,1)}, u32[]{:S(2)}) copy-start(bf16[2,3,133,512]{3,0,2,1:T(2,128)(2,1)} %param.10) | copy-start | bytes 2451460
Sparse Core Ops, SparseCore 0:
  9.2 136.9 all-gather.1
  207.7 249.5 reduce-scatter.1
where the time goes:
time: 467 us; the launch traced here: 464 us
  waiting for transfers between devices  250 us (54%)
  local copies, waits for them, and re-layouts  148 us (32%)
  other arithmetic  20.2 us (4%)
  matrix products  19.3 us (4%)
  between operations  14.9 us (3%)
  starting transfers between devices  11.5 us (2%)
    reduce_scatter x1, waiting for transfers between devices, body(): lax.psum_scatter(terms.astype(jnp.bfloat16), 'chan', scatter_dimension=1,...  250 us
    gather x2, local copies, waits for them, and re-layouts, toeplitz_long(): picked = jnp.take(filters, jnp.clip(lagged, 0, long_len - 1), axis=1)  124 us
    dot_general x1, matrix products, body(): jnp.dot(gated, lax.all_gather(out_weight, 'ctx', axis=1, tiled=True), pre...  14.2 us
    add x1, other arithmetic, short_filtering(): total + taps[offset][:, None, :] * extended[:, begin:begin + length, :].a...  10.1 us
  transfers between devices with their start and end apart: 4, of which 1 were waited for; matrix products, arithmetic and copies ran while one was open for 37% of the time, Pallas kernels for 0%

commit v1 on v0

v1 whole, which is shorter than its diff:
```python
import jax
import jax.numpy as jnp
from jax import lax
from jax.experimental import pallas as pl
from jax.experimental.pallas import tpu as pltpu
from jax.sharding import PartitionSpec as P

LANES = 128
HEAD = 144
F32 = jnp.float32
BF16 = jnp.bfloat16


def toeplitz_kernel(rows_ref, out_ref):
    long_len, width = LANES, rows_ref.shape[1]
    for g in range(rows_ref.shape[0]):
        wide = jnp.broadcast_to(rows_ref[g : g + 1, :], (long_len, width))
        band = pltpu.roll(wide, 0, 1, stride=1, stride_axis=0)
        out_ref[g * long_len : (g + 1) * long_len, :] = band.astype(BF16)


def toeplitz(long_filter):
    groups, long_len = long_filter.shape
    rows = jnp.pad(long_filter[:, ::-1].astype(F32), ((0, 0), (1, long_len - 1)))
    return pl.pallas_call(
        toeplitz_kernel,
        grid=(groups // 8,),
        in_specs=[pl.BlockSpec((8, 2 * long_len), lambda i: (i, 0))],
        out_specs=pl.BlockSpec((8 * long_len, 2 * long_len), lambda i: (i, 0)),
        out_shape=jax.ShapeDtypeStruct((groups * long_len, 2 * long_len), BF16),
        name="toeplitz",
    )(rows)


def conv_kernel(head_ref, body_ref, taps_ref, skip_ref, band_ref, out_ref, ext, prod):
    short_len = taps_ref.shape[1]
    tokens = body_ref.shape[1]
    blocks = tokens // LANES
    ext[:, :HEAD, :] = head_ref[...].astype(F32)
    ext[:, HEAD:, :] = body_ref[...].astype(F32)

    def short(s, begin):
        total = None
        for j in range(short_len):
            term = taps_ref[s, j : j + 1, :] * ext[s, begin + 16 - j : begin + 16 - j + LANES, :]
            total = term if total is None else total + term
        return total

    for n in range(blocks + 1):
        prod[n * LANES : (n + 1) * LANES, :] = (
            short(1, n * LANES) * short(2, n * LANES)
        ).astype(BF16)
    group = lax.broadcasted_iota(jnp.int32, (LANES, LANES), 1) // 16
    for n in range(blocks):
        window = prod[n * LANES : (n + 2) * LANES, :]
        every = jnp.dot(band_ref[...], window, preferred_element_type=F32)
        long_out = every[:LANES]
        for g in range(1, 8):
            long_out = jnp.where(group == g, every[g * LANES : (g + 1) * LANES], long_out)
        direct = prod[(n + 1) * LANES : (n + 2) * LANES, :].astype(F32)
        query = short(0, (n + 1) * LANES)
        out_ref[n * LANES : (n + 1) * LANES, :] = (
            query * (long_out + skip_ref[...] * direct)
        ).astype(BF16)


def gated_tokens(head, body, taps, skip, band):
    sets, tokens, channels = body.shape
    return pl.pallas_call(
        conv_kernel,
        grid=(channels // LANES,),
        in_specs=[
            pl.BlockSpec((sets, HEAD, LANES), lambda i: (0, 0, i)),
            pl.BlockSpec((sets, tokens, LANES), lambda i: (0, 0, i)),
            pl.BlockSpec((sets, taps.shape[1], LANES), lambda i: (0, 0, i)),
            pl.BlockSpec((1, LANES), lambda i: (0, i)),
            pl.BlockSpec((8 * LANES, 2 * LANES), lambda i: (i, 0)),
        ],
        out_specs=pl.BlockSpec((tokens, LANES), lambda i: (0, i)),
        out_shape=jax.ShapeDtypeStruct((tokens, channels), BF16),
        scratch_shapes=[
            pltpu.VMEM((sets, HEAD + tokens, LANES), F32),
            pltpu.VMEM((LANES + tokens, LANES), BF16),
        ],
        compiler_params=pltpu.CompilerParams(vmem_limit_bytes=48 * 1024 * 1024),
        name="conv",
    )(head, body, taps, skip, band)


def project_kernel(gated_ref, weights_ref, out_ref):
    total = None
    for k in range(gated_ref.shape[0]):
        term = jnp.dot(gated_ref[k], weights_ref[0, k, 0], preferred_element_type=F32)
        total = term if total is None else total + term
    out_ref[0] = total.astype(BF16)


def project(gated, weights):
    parts, tokens, depth = gated.shape
    width = weights.shape[-1]
    return pl.pallas_call(
        project_kernel,
        grid=(4,),
        in_specs=[
            pl.BlockSpec((parts, tokens, depth), lambda s: (0, 0, 0)),
            pl.BlockSpec((1, parts, 1, depth, width), lambda s: (s // 2, 0, s % 2, 0, 0)),
        ],
        out_specs=pl.BlockSpec((1, tokens, width), lambda s: (s, 0, 0)),
        out_shape=jax.ShapeDtypeStruct((4, tokens, width), BF16),
        compiler_params=pltpu.CompilerParams(vmem_limit_bytes=48 * 1024 * 1024),
        name="project",
    )(gated, weights)


def swapped_pairs():
    pairs = []
    for ctx in range(16):
        for chan in range(16):
            inner, ring = (ctx >> 1) & 3, (chan >> 1) & 3
            to_ctx = (ctx & 9) | (ring << 1)
            to_chan = (chan & 9) | (inner << 1)
            pairs.append((ctx * 16 + chan, to_ctx * 16 + to_chan))
    return pairs


def grouped(value, groups):
    return lax.all_to_all(
        value, "chan", split_axis=0, concat_axis=0, tiled=True, axis_index_groups=groups
    )


def pool_pieces(pool_tails):
    pool_dev, sets, tail, channels = pool_tails.shape
    rows = jnp.transpose(pool_tails, (1, 2, 0, 3)).reshape(sets * tail, pool_dev, channels)
    count = lax.axis_size("ctx")
    each = -(-(sets * tail) // count)
    rows = jnp.pad(rows, ((0, each * count - sets * tail), (0, 0), (0, 0)))
    return rows.reshape(count, each, pool_dev, channels)


def chosen_pieces(pieces, stripe_request, hit_holder, hit_block):
    count, _, pool_dev, _ = pieces.shape
    request = jnp.arange(hit_holder.shape[0], dtype=jnp.int32)
    ours = (stripe_request[:, None] == request[None, :]).astype(jnp.int32)
    holder = jnp.sum(ours * hit_holder[None, :], axis=1)
    block = jnp.sum(ours * hit_block[None, :], axis=1)
    select = jnp.logical_and(
        holder[:, None, None] == jnp.arange(count, dtype=jnp.int32)[None, :, None],
        block[:, None, None] == jnp.arange(pool_dev, dtype=jnp.int32)[None, None, :],
    ).astype(BF16)
    return jnp.einsum("dhb,hrbc->drc", select, pieces, preferred_element_type=F32).astype(BF16)


def exchanged(value):
    return lax.all_to_all(value, "ctx", split_axis=0, concat_axis=0, tiled=True)


def body(
    features,
    pool_tails,
    short_filter,
    long_filter,
    skip_gain,
    out_weight,
    stripe_request,
    hit_holder,
    hit_block,
):
    sets, tokens, channels = features.shape
    tail = pool_tails.shape[2]
    split = 2 * LANES
    my_index = lax.axis_index("ctx")
    rings = [[j | (r << 1) for r in range(4)] for j in (0, 1, 8, 9)]
    pairs = [[j | (r << 1) for j in (0, 1, 8, 9)] for r in range(4)]

    def spread(gated):
        return grouped(jnp.broadcast_to(gated, (4, *gated.shape)), rings)

    pieces = exchanged(pool_pieces(pool_tails))
    swapped = lax.ppermute(out_weight, ("ctx", "chan"), swapped_pairs())
    taps = jnp.transpose(short_filter, (1, 0, 2)).astype(F32)
    skip = skip_gain[None, :]
    band = toeplitz(long_filter)
    late = gated_tokens(
        features[:, split - HEAD : split, :], features[:, split:, :], taps, skip, band
    )
    previous = lax.ppermute(
        features[:, tokens - HEAD :, :], "ctx", [(i, i + 1) for i in range(15)]
    )
    pulled = exchanged(chosen_pieces(pieces, stripe_request, hit_holder, hit_block))
    swapped, pulled, late = lax.optimization_barrier((swapped, pulled, late))
    weights = lax.all_gather(swapped, "ctx", axis=0, tiled=True)
    weights = weights.reshape(2, 4, 2, *out_weight.shape)
    late = spread(late)
    pulled = pulled.reshape(-1, channels)[: sets * tail].reshape(sets, tail, channels)

    order = jnp.arange(stripe_request.shape[0], dtype=jnp.int32)
    request = jnp.sum(jnp.where(order == my_index, stripe_request, 0))
    earlier = jnp.sum(jnp.where(order == my_index - 1, stripe_request, 0))
    starting = jnp.logical_or(my_index == 0, earlier != request)
    pulled = jnp.pad(pulled, ((0, 0), (HEAD - tail, 0), (0, 0)))
    head = jnp.where(starting, pulled, previous)
    early = gated_tokens(head, features[:, :split, :], taps, skip, band)
    early, late = lax.optimization_barrier((early, late))
    early, partial = lax.optimization_barrier((spread(early), project(late, weights)))
    late = grouped(partial, pairs)
    early, late = lax.optimization_barrier((project(early, weights), late))
    early = grouped(early, pairs)

    def mixed(arrived):
        return jnp.sum(arrived.astype(F32), axis=0).astype(BF16)

    return jnp.concatenate([mixed(early), mixed(late)], axis=0)


def solution(mesh):
    return jax.shard_map(
        body,
        mesh=mesh,
        in_specs=(
            P(None, "ctx", "chan"),
            P("ctx", None, None, "chan"),
            P(None, None, "chan"),
            P("chan", None),
            P("chan"),
            P("chan", "ctx"),
            P(),
            P(),
            P(),
        ),
        out_specs=P("ctx", "chan"),
        check_vma=False,
    )
```

time: 467 us -> 214 us (0.46)
  waiting for transfers between devices: 250 us -> 83.1 us
  local copies, waits for them, and re-layouts: 148 us -> 13.1 us
  starting transfers between devices: 11.5 us -> 69 us
  Pallas kernels: 0 us -> 25.7 us
  matrix products: 19.3 us -> 0.39 us
  other arithmetic: 20.2 us -> 6.13 us
    reduce_scatter x1 -> x0, waiting for transfers between devices: 250 us -> none  [body(): lax.psum_scatter(terms.astype(jnp.bfloat16), 'chan', scatter_dimension=1,...]
    gather x4 -> x0, local copies, waits for them, and re-layouts: 126 us -> none  [the longest x2 124 us: toeplitz_long(): picked = jnp.take(filters, jnp.clip(lagged, 0, long_len - 1), axis=1)]
    all_to_all x1 -> x6, waiting for transfers between devices: 0.01 us -> 73.6 us  [the longest x4 52.1 us: grouped(): lax.all_to_all(value, 'chan', split_axis=0, concat_axis=0, tiled=True, ax...]
    all_to_all x1 -> x6, starting transfers between devices: 7.69 us -> 59.8 us  [the longest x4 46.5 us: grouped(): lax.all_to_all(value, 'chan', split_axis=0, concat_axis=0, tiled=True, ax...]
    pallas_call x0 -> x5, Pallas kernels: none -> 25.7 us  [the longest x2 15 us: project(): pl.pallas_call(project_kernel, grid=(4,), in_specs=[pl.BlockSpec((parts,...]
    dot_general x3 -> x1, matrix products: 19.3 us -> 0.39 us  [chosen_pieces(): jnp.einsum('dhb,hrbc->drc', select, pieces, preferred_element_type=F32)]
    add x2 -> x0, other arithmetic: 10.1 us -> none  [the longest x1 10.1 us: short_filtering(): total + taps[offset][:, None, :] * extended[:, begin:begin + length, :].a...]
    ppermute x1 -> x2, waiting for transfers between devices: 0.01 us -> 9.41 us  [the longest x1 9.41 us: body(): lax.ppermute(features[:, tokens - HEAD:, :], 'ctx', [(i, i + 1) for i in...]
  transfers between devices with their start and end apart: 4 -> 9, of which waited for: 1 -> 7; matrix products, arithmetic and copies ran while one was open for 37% -> 7% of each run, Pallas kernels for 0% -> 12%
where the time goes in v1:
time: 214 us; the launch traced here: 212 us
  waiting for transfers between devices  83.1 us (39%)
  starting transfers between devices  69 us (32%)
  Pallas kernels  25.7 us (12%)
  between operations  14.8 us (7%)
  local copies, waits for them, and re-layouts  13.1 us (6%)
  other arithmetic  6.13 us (3%)
    all_to_all x4, waiting for transfers between devices, grouped(): lax.all_to_all(value, 'chan', split_axis=0, concat_axis=0, tiled=True, ax...  52.1 us
    all_to_all x4, starting transfers between devices, grouped(): lax.all_to_all(value, 'chan', split_axis=0, concat_axis=0, tiled=True, ax...  46.5 us
    all_to_all x2, waiting for transfers between devices, exchanged(): return lax.all_to_all(value, 'ctx', split_axis=0, concat_axis=0, tiled=True)  21.5 us
    pallas_call x2, Pallas kernels, project(): pl.pallas_call(project_kernel, grid=(4,), in_specs=[pl.BlockSpec((parts,...  15 us
    all_to_all x2, starting transfers between devices, exchanged(): return lax.all_to_all(value, 'ctx', split_axis=0, concat_axis=0, tiled=True)  13.3 us
    ppermute x1, waiting for transfers between devices, body(): lax.ppermute(features[:, tokens - HEAD:, :], 'ctx', [(i, i + 1) for i in...  9.41 us
    pallas_call x2, Pallas kernels, gated_tokens(): pl.pallas_call(conv_kernel, grid=(channels // LANES,), in_specs=[pl.Block...  7.3 us
    ppermute x1, starting transfers between devices, body(): swapped = lax.ppermute(out_weight, ('ctx', 'chan'), swapped_pairs())  5.35 us
  transfers between devices with their start and end apart: 9, of which 7 were waited for; matrix products, arithmetic and copies ran while one was open for 7% of the time, Pallas kernels for 12%

profile of v1, /device:TPU:1, one launch (start us, length us, event | category | flops | bytes accessed | tf_op | source)
XLA Modules:
  0.0 212.2 jit_solution(14210342036834349067)
XLA Ops:
  6.5 0.0 copy-start.5
  6.5 2.7 %pad.14 = bf16[400,2,512]{2,1,0:T(2,128)(2,1)} pad(bf16[399,2,512]{2,1,0:T(2,128)(2,1)} %bitcast.23, bf16[]{:T(256)} %constant.18.clone.1), padding=0_1x0_0x0_0 | pad | bytes 1636354 | tf_op jit(solution)/shard_map/jit(_pad)/pad | solution.py:137
  9.2 0.0 copy-start.3
  9.2 7.0 %all-to-all-start = ((bf16[16,25,2,512]{3,2,1,0:T(2,128)(2,1)}), bf16[16,25,2,512]{3,2,1,0:T(2,128)(2,1)S(1)}, u32[]{:S(2)}, u32[]{:S(2)}) async-start(bf16[16,25,2,512]{3,2,1,0:T(2,128)(2,1)} %bitcast.21), calls=%async_computation | async-start | bytes 1638400 | tf_op jit(solution)/shard_map/all_to_all | solution.py:155
  16.3 5.3 %collective-permute-start = (bf16[512,512]{1,0:T(8,128)(2,1)}, bf16[512,512]{1,0:T(8,128)(2,1)}, u32[]{:S(2)}, u32[]{:S(2)}) collective-permute-start(bf16[512,512]{1,0:T(8,128)(2,1)} %param.14), channel_id=1, source_target_pairs={{0,0},{1,1},{2,32},{3,33},{4,64},{5,65},{6,96},{7,97},{8,8},{9,9},... | collective-permute-start | bytes 1572872 | tf_op jit(solution)/shard_map/ppermute | solution.py:180
  21.6 0.0 copy-done.5
  21.6 0.1 rev.3
  21.7 0.7 pad_convert_fusion.rows_ref
  22.4 3.4 %toeplitz.1.band_ref = bf16[4096,256]{1,0:T(8,128)(2,1)} custom-call(f32[32,256]{1,0:T(8,128)} %pad_convert_fusion.rows_ref), custom_call_target="tpu_custom_call" | custom-call | tf_op jit(solution)/shard_map/toeplitz/pallas_call | solution.py:25
  25.8 0.0 copy-done.3
  25.8 0.0 copy-start.6
  25.8 0.0 copy-start.7
  25.8 0.0 copy-start.8
  25.8 1.3 slice.16.body_ref
  27.1 0.0 copy-done.6
  27.1 0.0 copy-done.7
  27.1 0.0 copy-done.8
  27.1 0.0 copy-start.4
  27.1 0.1 select_reduce_fusion.1
  27.2 0.1 iota_compare_fusion
  27.3 2.3 %all-to-all-done = bf16[16,25,2,512]{3,2,1,0:T(2,128)(2,1)S(1)} async-done(((bf16[16,25,2,512]{3,2,1,0:T(2,128)(2,1)}), bf16[16,25,2,512]{3,2,1,0:T(2,128)(2,1)S(1)}, u32[]{:S(2)}, u32[]{:S(2)}) %all-to-all-start) | async-done | bytes 819232 | tf_op jit(solution)/shard_map/all_to_all | solution.py:155
  29.6 0.4 fusion
  30.0 0.0 copy-start
  30.0 0.0 copy-start.2
  30.0 1.0 copy.15
  31.0 6.3 %all-to-all-start.1 = ((bf16[16,25,512]{2,1,0:T(8,128)(2,1)}), bf16[16,25,512]{2,1,0:T(8,128)(2,1)S(1)}, u32[]{:S(2)}, u32[]{:S(2)}) async-start(bf16[16,25,512]{2,1,0:T(8,128)(2,1)} %copy.15), calls=%async_computation.1 | async-start | bytes 1048576 | tf_op jit(solution)/shard_map/all_to_all | solution.py:155
  37.3 0.0 all-gather.2.cloned.1.call-start
  37.3 0.0 copy-done.4
  37.3 0.0 copy-start.1
  37.4 2.1 fusion.8
  39.5 0.0 copy-done
  39.5 0.0 copy-done.2
  39.5 0.0 copy-done.1
  39.5 4.4 %conv.2 = bf16[512,512]{1,0:T(8,128)(2,1)S(1)} custom-call(bf16[3,144,512]{2,1,0:T(8,128)(2,1)S(1)} %get-tuple-element.27.head_ref, bf16[3,512,512]{2,1,0:T(8,128)(2,1)S(1)} %copy-done.1, f32[3,7,512]{2,1,0:T(8,128)S(1)} %convert_bitcast_fusion.taps_ref, f32[1,512]{1,0:T(1,128)S(1)} %bitcast.17, bf16[4096,256]{1,0:T(8,128)(2,1)S(1)} %copy-done), custom_call_target="tpu_custom_call" | custom-call | tf_op jit(solution)/shard_map/conv/pallas_call | solution.py:69
  43.9 0.0 collective-permute-done
  43.9 19.2 %all-to-all-done.1 = bf16[16,25,512]{2,1,0:T(8,128)(2,1)S(1)} async-done(((bf16[16,25,512]{2,1,0:T(8,128)(2,1)}), bf16[16,25,512]{2,1,0:T(8,128)(2,1)S(1)}, u32[]{:S(2)}, u32[]{:S(2)}) %all-to-all-start.1) | async-done | bytes 409632 | tf_op jit(solution)/shard_map/all_to_all | solution.py:155
  63.1 0.0 all-gather.2.cloned.1.call-update
  63.1 1.5 broadcast_in_dim.24
  64.6 8.3 %all-to-all-start.2 = ((bf16[4,512,512]{2,1,0:T(8,128)(2,1)}), bf16[4,512,512]{2,1,0:T(8,128)(2,1)}, u32[]{:S(2)}, u32[]{:S(2)}) async-start(bf16[4,512,512]{2,1,0:T(8,128)(2,1)} %broadcast_in_dim.24), calls=%async_computation.2 | async-start | bytes 4194304 | tf_op jit(solution)/shard_map/all_to_all | solution.py:127
  72.9 3.8 %collective-permute-start.1 = (bf16[3,144,512]{2,1,0:T(8,128)(2,1)}, bf16[3,144,512]{2,1,0:T(8,128)(2,1)}, u32[]{:S(2)}, u32[]{:S(2)}) collective-permute-start(bf16[3,144,512]{2,1,0:T(8,128)(2,1)} %get-tuple-element.28), channel_id=1, source_target_pairs={{0,16},{16,32},{32,48},{48,64},{64,80},{80,96},{96,112},{112,128},... | collective-permute-start | bytes 1327112 | tf_op jit(solution)/shard_map/ppermute | solution.py:187
  76.7 1.3 slice.19.body_ref
  78.0 0.6 fusion.7
  79.9 0.9 reshape.66
  80.8 1.1 reshape.67
  81.9 9.4 %collective-permute-done.1 = bf16[3,144,512]{2,1,0:T(8,128)(2,1)} collective-permute-done((bf16[3,144,512]{2,1,0:T(8,128)(2,1)}, bf16[3,144,512]{2,1,0:T(8,128)(2,1)}, u32[]{:S(2)}, u32[]{:S(2)}) %collective-permute-start.1) | collective-permute-done | bytes 442400 | tf_op jit(solution)/shard_map/ppermute | solution.py:187
  91.3 1.2 pad_select_fusion.head_ref
  92.5 2.9 %conv.3 = bf16[256,512]{1,0:T(8,128)(2,1)S(1)} custom-call(bf16[3,144,512]{2,1,0:T(8,128)(2,1)S(1)} %pad_select_fusion.head_ref, bf16[3,256,512]{2,1,0:T(8,128)(2,1)S(1)} %slice.19.body_ref, f32[3,7,512]{2,1,0:T(8,128)S(1)} %convert_bitcast_fusion.taps_ref, f32[1,512]{1,0:T(1,128)S(1)} %bitcast.18, bf16[4096,256]{1,0:T(8,128)(2,1)S(1)} %copy-done), custom_call_target="tpu_custom_call" | custom-call | tf_op jit(solution)/shard_map/conv/pallas_call | solution.py:69
  95.4 10.2 %all-to-all-done.2.gated_ref = bf16[4,512,512]{2,1,0:T(8,128)(2,1)} async-done(((bf16[4,512,512]{2,1,0:T(8,128)(2,1)}), bf16[4,512,512]{2,1,0:T(8,128)(2,1)}, u32[]{:S(2)}, u32[]{:S(2)}) %all-to-all-start.2) | async-done | bytes 2097184 | tf_op jit(solution)/shard_map/all_to_all | solution.py:127
  105.6 1.1 broadcast_in_dim.25
  106.8 19.5 %all-to-all-start.3 = ((bf16[4,256,512]{2,1,0:T(8,128)(2,1)}), bf16[4,256,512]{2,1,0:T(8,128)(2,1)S(1)}, u32[]{:S(2)}, u32[]{:S(2)}) async-start(bf16[4,256,512]{2,1,0:T(8,128)(2,1)} %broadcast_in_dim.25), calls=%async_computation.3 | async-start | bytes 2097152 | tf_op jit(solution)/shard_map/all_to_all | solution.py:127
  126.3 0.0 all-gather.2.cloned.1.call-done
  126.3 8.7 %project.2 = bf16[4,512,512]{2,1,0:T(8,128)(2,1)} custom-call(bf16[4,512,512]{2,1,0:T(8,128)(2,1)} %all-to-all-done.2.gated_ref, bf16[2,4,2,512,512]{4,3,2,1,0:T(8,128)(2,1)} %bitcast.19), custom_call_target="tpu_custom_call" | custom-call | tf_op jit(solution)/shard_map/project/pallas_call | solution.py:101
  135.0 9.1 %all-to-all-done.3.gated_ref = bf16[4,256,512]{2,1,0:T(8,128)(2,1)S(1)} async-done(((bf16[4,256,512]{2,1,0:T(8,128)(2,1)}), bf16[4,256,512]{2,1,0:T(8,128)(2,1)S(1)}, u32[]{:S(2)}, u32[]{:S(2)}) %all-to-all-start.3) | async-done | bytes 1048608 | tf_op jit(solution)/shard_map/all_to_all | solution.py:127
  144.1 15.1 %all-to-all-start.4 = ((bf16[4,512,512]{2,1,0:T(8,128)(2,1)}), bf16[4,512,512]{2,1,0:T(8,128)(2,1)S(1)}, u32[]{:S(2)}, u32[]{:S(2)}) async-start(bf16[4,512,512]{2,1,0:T(8,128)(2,1)} %project.2), calls=%async_computation.4 | async-start | bytes 4194304 | tf_op jit(solution)/shard_map/all_to_all | solution.py:127
  159.2 6.3 %project.3 = bf16[4,256,512]{2,1,0:T(8,128)(2,1)} custom-call(bf16[4,256,512]{2,1,0:T(8,128)(2,1)S(1)} %all-to-all-done.3.gated_ref, bf16[2,4,2,512,512]{4,3,2,1,0:T(8,128)(2,1)} %bitcast.20), custom_call_target="tpu_custom_call" | custom-call | tf_op jit(solution)/shard_map/project/pallas_call | solution.py:101
  165.5 19.5 %all-to-all-done.4 = bf16[4,512,512]{2,1,0:T(8,128)(2,1)S(1)} async-done(((bf16[4,512,512]{2,1,0:T(8,128)(2,1)}), bf16[4,512,512]{2,1,0:T(8,128)(2,1)S(1)}, u32[]{:S(2)}, u32[]{:S(2)}) %all-to-all-start.4) | async-done | bytes 2097184 | tf_op jit(solution)/shard_map/all_to_all | solution.py:127
  185.1 3.5 %all-to-all-start.5 = ((bf16[4,256,512]{2,1,0:T(8,128)(2,1)}), bf16[4,256,512]{2,1,0:T(8,128)(2,1)S(1)}, u32[]{:S(2)}, u32[]{:S(2)}) async-start(bf16[4,256,512]{2,1,0:T(8,128)(2,1)} %project.3), calls=%async_computation.5 | async-start | bytes 2097152 | tf_op jit(solution)/shard_map/all_to_all | solution.py:127
  188.6 1.2 reduce_sum.65
  189.8 13.3 %all-to-all-done.5 = bf16[4,256,512]{2,1,0:T(8,128)(2,1)S(1)} async-done(((bf16[4,256,512]{2,1,0:T(8,128)(2,1)}), bf16[4,256,512]{2,1,0:T(8,128)(2,1)S(1)}, u32[]{:S(2)}, u32[]{:S(2)}) %all-to-all-start.5) | async-done | bytes 1048608 | tf_op jit(solution)/shard_map/all_to_all | solution.py:127
  203.1 0.2 reduce_sum.64
  203.4 2.0 pad_maximum_fusion
  (2 shorter events, 0.0 us)
Async XLA Ops:
  6.5 15.1 %copy-start.5 = (bf16[32,128]{1,0:T(8,128)(2,1)S(1)}, bf16[32,128]{1,0:T(8,128)(2,1)}, u32[]{:S(2)}) copy-start(bf16[32,128]{1,0:T(8,128)(2,1)} %param.12) | copy-start | bytes 24580
  9.2 16.6 %copy-start.3 = (bf16[3,768,512]{2,1,0:T(8,128)(2,1)S(1)}, bf16[3,768,512]{2,1,0:T(8,128)(2,1)}, u32[]{:S(2)}) copy-start(bf16[3,768,512]{2,1,0:T(8,128)(2,1)} %param.9) | copy-start | bytes 7077892
  9.2 20.4 %all-to-all-start = ((bf16[16,25,2,512]{3,2,1,0:T(2,128)(2,1)}), bf16[16,25,2,512]{3,2,1,0:T(2,128)(2,1)S(1)}, u32[]{:S(2)}, u32[]{:S(2)}) async-start(bf16[16,25,2,512]{3,2,1,0:T(2,128)(2,1)} %bitcast.21), calls=%async_computation | async-start | bytes 1638400 | tf_op jit(solution)/shard_map/all_to_all | solution.py:155
  16.3 27.6 %collective-permute-start = (bf16[512,512]{1,0:T(8,128)(2,1)}, bf16[512,512]{1,0:T(8,128)(2,1)}, u32[]{:S(2)}, u32[]{:S(2)}) collective-permute-start(bf16[512,512]{1,0:T(8,128)(2,1)} %param.14), channel_id=1, source_target_pairs={{0,0},{1,1},{2,32},{3,33},{4,64},{5,65},{6,96},{7,97},{8,8},{9,9},... | collective-permute-start | bytes 1572872 | tf_op jit(solution)/shard_map/ppermute | solution.py:180
  25.8 1.3 copy-start.6
  25.8 1.3 copy-start.7
  25.8 1.3 copy-start.8
  27.1 10.3 %copy-start.4 = (bf16[7,3,512]{2,0,1:T(8,128)(2,1)S(1)}, bf16[7,3,512]{2,0,1:T(8,128)(2,1)}, u32[]{:S(2)}) copy-start(bf16[7,3,512]{2,0,1:T(8,128)(2,1)} %param.11) | copy-start | bytes 64516
  30.0 9.5 %copy-start = (bf16[4096,256]{1,0:T(8,128)(2,1)S(1)}, bf16[4096,256]{1,0:T(8,128)(2,1)}, u32[]{:S(2)}) copy-start(bf16[4096,256]{1,0:T(8,128)(2,1)} %toeplitz.1.band_ref) | copy-start | bytes 6291460
  30.0 9.5 %copy-start.2 = (f32[512]{0:T(512)S(1)}, f32[512]{0:T(512)}, u32[]{:S(2)}) copy-start(f32[512]{0:T(512)} %param.13) | copy-start | bytes 6148
  31.0 32.0 %all-to-all-start.1 = ((bf16[16,25,512]{2,1,0:T(8,128)(2,1)}), bf16[16,25,512]{2,1,0:T(8,128)(2,1)S(1)}, u32[]{:S(2)}, u32[]{:S(2)}) async-start(bf16[16,25,512]{2,1,0:T(8,128)(2,1)} %copy.15), calls=%async_computation.1 | async-start | bytes 1048576 | tf_op jit(solution)/shard_map/all_to_all | solution.py:155
  37.3 89.0 %all-gather.2.cloned.1.call-start = ((), (), s32[]{:S(2)}) async-start(), calls=%async_computation.6 | async-start | bytes 8912896 | tf_op jit(solution)/shard_map/all_gather | solution.py:192
  37.3 2.1 %copy-start.1 = (bf16[3,512,512]{2,1,0:T(8,128)(2,1)S(1)}, bf16[3,512,512]{2,1,0:T(8,128)(2,1)}, u32[]{:S(2)}) copy-start(bf16[3,512,512]{2,1,0:T(8,128)(2,1)} %slice.16.body_ref) | copy-start | bytes 4718596
  64.6 41.0 %all-to-all-start.2 = ((bf16[4,512,512]{2,1,0:T(8,128)(2,1)}), bf16[4,512,512]{2,1,0:T(8,128)(2,1)}, u32[]{:S(2)}, u32[]{:S(2)}) async-start(bf16[4,512,512]{2,1,0:T(8,128)(2,1)} %broadcast_in_dim.24), calls=%async_computation.2 | async-start | bytes 4194304 | tf_op jit(solution)/shard_map/all_to_all | solution.py:127
  72.9 18.4 %collective-permute-start.1 = (bf16[3,144,512]{2,1,0:T(8,128)(2,1)}, bf16[3,144,512]{2,1,0:T(8,128)(2,1)}, u32[]{:S(2)}, u32[]{:S(2)}) collective-permute-start(bf16[3,144,512]{2,1,0:T(8,128)(2,1)} %get-tuple-element.28), channel_id=1, source_target_pairs={{0,16},{16,32},{32,48},{48,64},{64,80},{80,96},{96,112},{112,128},... | collective-permute-start | bytes 1327112 | tf_op jit(solution)/shard_map/ppermute | solution.py:187
  106.8 37.3 %all-to-all-start.3 = ((bf16[4,256,512]{2,1,0:T(8,128)(2,1)}), bf16[4,256,512]{2,1,0:T(8,128)(2,1)S(1)}, u32[]{:S(2)}, u32[]{:S(2)}) async-start(bf16[4,256,512]{2,1,0:T(8,128)(2,1)} %broadcast_in_dim.25), calls=%async_computation.3 | async-start | bytes 2097152 | tf_op jit(solution)/shard_map/all_to_all | solution.py:127
  144.1 41.0 %all-to-all-start.4 = ((bf16[4,512,512]{2,1,0:T(8,128)(2,1)}), bf16[4,512,512]{2,1,0:T(8,128)(2,1)S(1)}, u32[]{:S(2)}, u32[]{:S(2)}) async-start(bf16[4,512,512]{2,1,0:T(8,128)(2,1)} %project.2), calls=%async_computation.4 | async-start | bytes 4194304 | tf_op jit(solution)/shard_map/all_to_all | solution.py:127
  185.1 18.1 %all-to-all-start.5 = ((bf16[4,256,512]{2,1,0:T(8,128)(2,1)}), bf16[4,256,512]{2,1,0:T(8,128)(2,1)S(1)}, u32[]{:S(2)}, u32[]{:S(2)}) async-start(bf16[4,256,512]{2,1,0:T(8,128)(2,1)} %project.3), calls=%async_computation.5 | async-start | bytes 2097152 | tf_op jit(solution)/shard_map/all_to_all | solution.py:127
Sparse Core Ops, SparseCore 0:
  63.2 60.7 all-gather.1

commit v2 on v1

--- a/solution.py
+++ b/solution.py
@@ -87,29 +87,35 @@
     )(head, body, taps, skip, band)
 
 
-def project_kernel(gated_ref, weights_ref, out_ref):
-    total = None
-    for k in range(gated_ref.shape[0]):
-        term = jnp.dot(gated_ref[k], weights_ref[0, k, 0], preferred_element_type=F32)
-        total = term if total is None else total + term
-    out_ref[0] = total.astype(BF16)
-
-
-def project(gated, weights):
-    parts, tokens, depth = gated.shape
+def project_kernel(side_ref, *refs):
+    weights_ref, out_ref = refs[-2:]
+    begin = 0
+    for gated_ref in refs[:-2]:
+        total = None
+        for k in range(gated_ref.shape[0]):
+            term = jnp.dot(gated_ref[k], weights_ref[0, k, 0], preferred_element_type=F32)
+            total = term if total is None else total + term
+        out_ref[0, begin : begin + gated_ref.shape[1], :] = total.astype(BF16)
+        begin += gated_ref.shape[1]
+
+
+def project(runs, weights, side):
+    parts, _, depth = runs[0].shape
+    tokens = sum(run.shape[1] for run in runs)
     width = weights.shape[-1]
     return pl.pallas_call(
         project_kernel,
-        grid=(4,),
-        in_specs=[
-            pl.BlockSpec((parts, tokens, depth), lambda s: (0, 0, 0)),
-            pl.BlockSpec((1, parts, 1, depth, width), lambda s: (s // 2, 0, s % 2, 0, 0)),
-        ],
-        out_specs=pl.BlockSpec((1, tokens, width), lambda s: (s, 0, 0)),
-        out_shape=jax.ShapeDtypeStruct((4, tokens, width), BF16),
+        grid_spec=pltpu.PrefetchScalarGridSpec(
+            num_scalar_prefetch=1,
+            grid=(2,),
+            in_specs=[pl.BlockSpec(run.shape, lambda s, side: (0, 0, 0)) for run in runs]
+            + [pl.BlockSpec((1, parts, 1, depth, width), lambda s, side: (side[0], 0, s, 0, 0))],
+            out_specs=pl.BlockSpec((1, tokens, width), lambda s, side: (s, 0, 0)),
+        ),
+        out_shape=jax.ShapeDtypeStruct((2, tokens, width), BF16),
         compiler_params=pltpu.CompilerParams(vmem_limit_bytes=48 * 1024 * 1024),
         name="project",
-    )(gated, weights)
+    )(jnp.reshape(side, (1,)).astype(jnp.int32), *runs, weights)
 
 
 def swapped_pairs():
@@ -171,7 +177,6 @@
     split = 2 * LANES
     my_index = lax.axis_index("ctx")
     rings = [[j | (r << 1) for r in range(4)] for j in (0, 1, 8, 9)]
-    pairs = [[j | (r << 1) for j in (0, 1, 8, 9)] for r in range(4)]
 
     def spread(gated):
         return grouped(jnp.broadcast_to(gated, (4, *gated.shape)), rings)
@@ -202,15 +207,35 @@
     head = jnp.where(starting, pulled, previous)
     early = gated_tokens(head, features[:, :split, :], taps, skip, band)
     early, late = lax.optimization_barrier((early, late))
-    early, partial = lax.optimization_barrier((spread(early), project(late, weights)))
-    late = grouped(partial, pairs)
-    early, late = lax.optimization_barrier((project(early, weights), late))
-    early = grouped(early, pairs)
-
-    def mixed(arrived):
-        return jnp.sum(arrived.astype(F32), axis=0).astype(BF16)
-
-    return jnp.concatenate([mixed(early), mixed(late)], axis=0)
+    early, late = [spread(early)], [late]
+
+    chan = lax.axis_index("chan")
+    high, low = chan >> 3, chan & 1
+
+    def flipped(value, bit):
+        return lax.ppermute(value, "chan", [(j, j ^ bit) for j in range(16)])
+
+    def halves(kept, came):
+        kept = kept.astype(F32) + came.astype(F32)
+        mine = jnp.where(low == 0, kept[0], kept[1])
+        other = jnp.where(low == 0, kept[1], kept[0])
+        return mine, other.astype(BF16)
+
+    def rounded(mine, came):
+        return (mine + came.astype(F32)).astype(BF16)
+
+    late_came = flipped(project(late, weights, 1 - high), 8)
+    late_kept = project(late, weights, high)
+    early, late_kept = lax.optimization_barrier((early, late_kept))
+    early_came = flipped(project(early, weights, 1 - high), 8)
+    late_mine, late_other = halves(late_kept, late_came)
+    early, late_other = lax.optimization_barrier((early, late_other))
+    late_came = flipped(late_other, 1)
+    early_mine, early_other = halves(project(early, weights, high), early_came)
+    early_came = flipped(early_other, 1)
+    return jnp.concatenate(
+        [rounded(early_mine, early_came), rounded(late_mine, late_came)], axis=0
+    )
 
 
 def solution(mesh):

time: 214 us -> 190 us (0.89)
  waiting for transfers between devices: 83.1 us -> 60.6 us
    all_to_all x4 -> x2, waiting for transfers between devices: 52.1 us -> 17.1 us  [grouped(): lax.all_to_all(value, 'chan', split_axis=0, concat_axis=0, tiled=True, ax...]
    all_to_all x4 -> x2, starting transfers between devices: 46.5 us -> 28 us  [grouped(): lax.all_to_all(value, 'chan', split_axis=0, concat_axis=0, tiled=True, ax...]
    ppermute x0 -> x4, starting transfers between devices: none -> 17.7 us  [flipped(): return lax.ppermute(value, 'chan', [(j, j ^ bit) for j in range(16)])]
    ppermute x0 -> x4, waiting for transfers between devices: none -> 13 us  [flipped(): return lax.ppermute(value, 'chan', [(j, j ^ bit) for j in range(16)])]
    pallas_call x2 -> x4, Pallas kernels: 15 us -> 15.6 us  [project(): pl.pallas_call(project_kernel, grid_spec=pltpu.PrefetchScalarGridSpec(num...]
  transfers between devices with their start and end apart: 9 -> 11, of which waited for: 7 -> 8; matrix products, arithmetic and copies ran while one was open for 7% -> 8% of each run, Pallas kernels for 12% -> 14%
where the time goes in v2:
time: 190 us; the launch traced here: 189 us
  starting transfers between devices  68.5 us (36%)
  waiting for transfers between devices  60.6 us (32%)
  Pallas kernels  26.3 us (14%)
  between operations  14.9 us (8%)
  local copies, waits for them, and re-layouts  13.2 us (7%)
  other arithmetic  4.89 us (3%)
    all_to_all x2, starting transfers between devices, grouped(): lax.all_to_all(value, 'chan', split_axis=0, concat_axis=0, tiled=True, ax...  28 us
    all_to_all x2, waiting for transfers between devices, exchanged(): return lax.all_to_all(value, 'ctx', split_axis=0, concat_axis=0, tiled=True)  21.3 us
    ppermute x4, starting transfers between devices, flipped(): return lax.ppermute(value, 'chan', [(j, j ^ bit) for j in range(16)])  17.7 us
    all_to_all x2, waiting for transfers between devices, grouped(): lax.all_to_all(value, 'chan', split_axis=0, concat_axis=0, tiled=True, ax...  17.1 us
    pallas_call x4, Pallas kernels, project(): pl.pallas_call(project_kernel, grid_spec=pltpu.PrefetchScalarGridSpec(num...  15.6 us
    all_to_all x2, starting transfers between devices, exchanged(): return lax.all_to_all(value, 'ctx', split_axis=0, concat_axis=0, tiled=True)  13.5 us
    ppermute x4, waiting for transfers between devices, flipped(): return lax.ppermute(value, 'chan', [(j, j ^ bit) for j in range(16)])  13 us
    ppermute x1, waiting for transfers between devices, body(): lax.ppermute(features[:, tokens - HEAD:, :], 'ctx', [(i, i + 1) for i in...  9.3 us
  transfers between devices with their start and end apart: 11, of which 8 were waited for; matrix products, arithmetic and copies ran while one was open for 8% of the time, Pallas kernels for 14%

profile of v2, /device:TPU:1, one launch (start us, length us, event | category | flops | bytes accessed | tf_op | source)
XLA Modules:
  0.0 188.8 jit_solution(16788902972367160774)
XLA Ops:
  6.5 2.8 %pad.14 = bf16[400,2,512]{2,1,0:T(2,128)(2,1)} pad(bf16[399,2,512]{2,1,0:T(2,128)(2,1)} %bitcast.39, bf16[]{:T(256)} %constant.20.clone.1), padding=0_1x0_0x0_0 | pad | bytes 1636354 | tf_op jit(solution)/shard_map/jit(_pad)/pad | solution.py:143
  9.4 7.0 %all-to-all-start = ((bf16[16,25,2,512]{3,2,1,0:T(2,128)(2,1)}), bf16[16,25,2,512]{3,2,1,0:T(2,128)(2,1)S(1)}, u32[]{:S(2)}, u32[]{:S(2)}) async-start(bf16[16,25,2,512]{3,2,1,0:T(2,128)(2,1)} %bitcast.37), calls=%async_computation | async-start | bytes 1638400 | tf_op jit(solution)/shard_map/all_to_all | solution.py:161
  16.4 0.0 copy-start.7
  16.4 0.0 copy-start.8
  16.4 5.5 %collective-permute-start = (bf16[512,512]{1,0:T(8,128)(2,1)}, bf16[512,512]{1,0:T(8,128)(2,1)}, u32[]{:S(2)}, u32[]{:S(2)}) collective-permute-start(bf16[512,512]{1,0:T(8,128)(2,1)} %param.14), channel_id=1, source_target_pairs={{0,0},{1,1},{2,32},{3,33},{4,64},{5,65},{6,96},{7,97},{8,8},{9,9},... | collective-permute-start | bytes 1572872 | tf_op jit(solution)/shard_map/ppermute | solution.py:185
  21.9 0.0 copy-done.3
  21.9 1.3 slice.32.body_ref
  23.2 0.0 copy-done.5
  23.2 0.1 rev.3
  23.3 0.7 pad_convert_fusion.rows_ref
  24.0 3.4 %toeplitz.1.band_ref = bf16[4096,256]{1,0:T(8,128)(2,1)} custom-call(f32[32,256]{1,0:T(8,128)} %pad_convert_fusion.rows_ref), custom_call_target="tpu_custom_call" | custom-call | tf_op jit(solution)/shard_map/toeplitz/pallas_call | solution.py:25
  27.4 0.0 copy-done.6
  27.4 0.0 copy-done.7
  27.4 0.0 copy-done.8
  27.4 0.0 copy-start.4
  27.4 0.1 select_reduce_fusion.1
  27.5 0.1 iota_compare_fusion
  27.6 2.2 %all-to-all-done = bf16[16,25,2,512]{3,2,1,0:T(2,128)(2,1)S(1)} async-done(((bf16[16,25,2,512]{3,2,1,0:T(2,128)(2,1)}), bf16[16,25,2,512]{3,2,1,0:T(2,128)(2,1)S(1)}, u32[]{:S(2)}, u32[]{:S(2)}) %all-to-all-start) | async-done | bytes 819232 | tf_op jit(solution)/shard_map/all_to_all | solution.py:161
  29.7 0.4 fusion
  30.1 0.0 copy-start
  30.1 0.0 copy-start.2
  30.2 1.0 copy.15
  31.2 6.4 %all-to-all-start.1 = ((bf16[16,25,512]{2,1,0:T(8,128)(2,1)}), bf16[16,25,512]{2,1,0:T(8,128)(2,1)S(1)}, u32[]{:S(2)}, u32[]{:S(2)}) async-start(bf16[16,25,512]{2,1,0:T(8,128)(2,1)} %copy.15), calls=%async_computation.1 | async-start | bytes 1048576 | tf_op jit(solution)/shard_map/all_to_all | solution.py:161
  37.6 0.0 all-gather.2.cloned.1.call-start
  37.7 0.0 copy-done.4
  37.7 0.0 copy-start.1
  37.7 2.1 %fusion.12 = (bf16[3,144,512]{2,1,0:T(8,128)(2,1)S(1)}, bf16[3,144,512]{2,1,0:T(8,128)(2,1)}) fusion(bf16[3,768,512]{2,1,0:T(8,128)(2,1)} %param.9), kind=kLoop, calls=%fused_computation.30 | loop fusion | bytes 1769472 | tf_op jit(solution)/shard_map/slice | solution.py:190
  39.8 4.4 %conv.2 = bf16[512,512]{1,0:T(8,128)(2,1)S(1)} custom-call(bf16[3,144,512]{2,1,0:T(8,128)(2,1)S(1)} %get-tuple-element.27.head_ref, bf16[3,512,512]{2,1,0:T(8,128)(2,1)S(1)} %copy-done.1, f32[3,7,512]{2,1,0:T(8,128)S(1)} %convert_bitcast_fusion.taps_ref, f32[1,512]{1,0:T(1,128)S(1)} %bitcast.31, bf16[4096,256]{1,0:T(8,128)(2,1)S(1)} %copy-done), custom_call_target="tpu_custom_call" | custom-call | tf_op jit(solution)/shard_map/conv/pallas_call | solution.py:69
  44.2 0.0 collective-permute-done
  44.2 19.1 %all-to-all-done.1 = bf16[16,25,512]{2,1,0:T(8,128)(2,1)S(1)} async-done(((bf16[16,25,512]{2,1,0:T(8,128)(2,1)}), bf16[16,25,512]{2,1,0:T(8,128)(2,1)S(1)}, u32[]{:S(2)}, u32[]{:S(2)}) %all-to-all-start.1) | async-done | bytes 409632 | tf_op jit(solution)/shard_map/all_to_all | solution.py:161
  63.3 0.0 all-gather.2.cloned.1.call-update
  63.3 1.5 broadcast_in_dim.24
  64.8 8.5 %all-to-all-start.2 = ((bf16[4,512,512]{2,1,0:T(8,128)(2,1)}), bf16[4,512,512]{2,1,0:T(8,128)(2,1)}, u32[]{:S(2)}, u32[]{:S(2)}) async-start(bf16[4,512,512]{2,1,0:T(8,128)(2,1)} %broadcast_in_dim.24), calls=%async_computation.2 | async-start | bytes 4194304 | tf_op jit(solution)/shard_map/all_to_all | solution.py:133
  73.3 3.7 %collective-permute-start.1 = (bf16[3,144,512]{2,1,0:T(8,128)(2,1)}, bf16[3,144,512]{2,1,0:T(8,128)(2,1)}, u32[]{:S(2)}, u32[]{:S(2)}) collective-permute-start(bf16[3,144,512]{2,1,0:T(8,128)(2,1)} %get-tuple-element.28), channel_id=1, source_target_pairs={{0,16},{16,32},{32,48},{48,64},{64,80},{80,96},{96,112},{112,128},... | collective-permute-start | bytes 1327112 | tf_op jit(solution)/shard_map/ppermute | solution.py:192
  77.0 1.3 slice.35.body_ref
  78.4 0.7 fusion.11
  80.3 0.9 reshape.85
  81.2 1.1 reshape.86
  82.3 9.3 %collective-permute-done.1 = bf16[3,144,512]{2,1,0:T(8,128)(2,1)} collective-permute-done((bf16[3,144,512]{2,1,0:T(8,128)(2,1)}, bf16[3,144,512]{2,1,0:T(8,128)(2,1)}, u32[]{:S(2)}, u32[]{:S(2)}) %collective-permute-start.1) | collective-permute-done | bytes 442400 | tf_op jit(solution)/shard_map/ppermute | solution.py:192
  91.6 0.2 pad_select_fusion.head_ref
  91.8 2.9 %conv.3 = bf16[256,512]{1,0:T(8,128)(2,1)S(1)} custom-call(bf16[3,144,512]{2,1,0:T(8,128)(2,1)S(1)} %pad_select_fusion.head_ref, bf16[3,256,512]{2,1,0:T(8,128)(2,1)S(1)} %slice.35.body_ref, f32[3,7,512]{2,1,0:T(8,128)S(1)} %convert_bitcast_fusion.taps_ref, f32[1,512]{1,0:T(1,128)S(1)} %bitcast.32, bf16[4096,256]{1,0:T(8,128)(2,1)S(1)} %copy-done), custom_call_target="tpu_custom_call" | custom-call | tf_op jit(solution)/shard_map/conv/pallas_call | solution.py:69
  94.7 11.3 %all-to-all-done.2.refs_0_ = bf16[4,512,512]{2,1,0:T(8,128)(2,1)} async-done(((bf16[4,512,512]{2,1,0:T(8,128)(2,1)}), bf16[4,512,512]{2,1,0:T(8,128)(2,1)}, u32[]{:S(2)}, u32[]{:S(2)}) %all-to-all-start.2) | async-done | bytes 2097184 | tf_op jit(solution)/shard_map/all_to_all | solution.py:133
  106.0 1.1 broadcast_in_dim.25
  107.1 19.6 %all-to-all-start.3 = ((bf16[4,256,512]{2,1,0:T(8,128)(2,1)}), bf16[4,256,512]{2,1,0:T(8,128)(2,1)S(1)}, u32[]{:S(2)}, u32[]{:S(2)}) async-start(bf16[4,256,512]{2,1,0:T(8,128)(2,1)} %broadcast_in_dim.25), calls=%async_computation.3 | async-start | bytes 2097152 | tf_op jit(solution)/shard_map/all_to_all | solution.py:133
  126.7 4.7 %project.5 = bf16[2,512,512]{2,1,0:T(8,128)(2,1)S(1)} custom-call(s32[1]{0:T(128)} %bitcast.10.side_ref, bf16[4,512,512]{2,1,0:T(8,128)(2,1)} %all-to-all-done.2.refs_0_, bf16[2,4,2,512,512]{4,3,2,1,0:T(8,128)(2,1)} %bitcast.33), custom_call_target="tpu_custom_call" | custom-call | tf_op jit(solution)/shard_map/project/pallas_call | solution.py:106
  131.4 2.5 %collective-permute-start.2 = (bf16[2,512,512]{2,1,0:T(8,128)(2,1)S(1)}, bf16[2,512,512]{2,1,0:T(8,128)(2,1)}, u32[]{:S(2)}, u32[]{:S(2)}) collective-permute-start(bf16[2,512,512]{2,1,0:T(8,128)(2,1)S(1)} %project.5), channel_id=1, source_target_pairs={{0,8},{1,9},{2,10},{3,11},{4,12},{5,13},{6,14},{7,15},{8,0},{9,1},... | collective-permute-start | bytes 3145736 | tf_op jit(solution)/shard_map/ppermute | solution.py:216
  133.9 4.7 %project.4 = bf16[2,512,512]{2,1,0:T(8,128)(2,1)S(1)} custom-call(s32[1]{0:T(128)} %bitcast.side_ref, bf16[4,512,512]{2,1,0:T(8,128)(2,1)} %all-to-all-done.2.refs_0_, bf16[2,4,2,512,512]{4,3,2,1,0:T(8,128)(2,1)} %bitcast.34), custom_call_target="tpu_custom_call" | custom-call | tf_op jit(solution)/shard_map/project/pallas_call | solution.py:106
  138.7 5.8 %all-to-all-done.3.refs_0_ = bf16[4,256,512]{2,1,0:T(8,128)(2,1)S(1)} async-done(((bf16[4,256,512]{2,1,0:T(8,128)(2,1)}), bf16[4,256,512]{2,1,0:T(8,128)(2,1)S(1)}, u32[]{:S(2)}, u32[]{:S(2)}) %all-to-all-start.3) | async-done | bytes 1048608 | tf_op jit(solution)/shard_map/all_to_all | solution.py:133
  144.5 3.0 %project.7 = bf16[2,256,512]{2,1,0:T(8,128)(2,1)S(1)} custom-call(s32[1]{0:T(128)} %bitcast.10.side_ref, bf16[4,256,512]{2,1,0:T(8,128)(2,1)S(1)} %all-to-all-done.3.refs_0_, bf16[2,4,2,512,512]{4,3,2,1,0:T(8,128)(2,1)} %bitcast.35), custom_call_target="tpu_custom_call" | custom-call | tf_op jit(solution)/shard_map/project/pallas_call | solution.py:106
  147.5 2.5 %collective-permute-start.3 = (bf16[2,256,512]{2,1,0:T(8,128)(2,1)S(1)}, bf16[2,256,512]{2,1,0:T(8,128)(2,1)S(1)}, u32[]{:S(2)}, u32[]{:S(2)}) collective-permute-start(bf16[2,256,512]{2,1,0:T(8,128)(2,1)S(1)} %project.7), channel_id=1, source_target_pairs={{0,8},{1,9},{2,10},{3,11},{4,12},{5,13},{6,14},{7,15},{8,0},{9,1},... | collective-permute-start | bytes 1572872 | tf_op jit(solution)/shard_map/ppermute | solution.py:216
  150.0 5.9 %collective-permute-done.2 = bf16[2,512,512]{2,1,0:T(8,128)(2,1)} collective-permute-done((bf16[2,512,512]{2,1,0:T(8,128)(2,1)S(1)}, bf16[2,512,512]{2,1,0:T(8,128)(2,1)}, u32[]{:S(2)}, u32[]{:S(2)}) %collective-permute-start.2) | collective-permute-done | bytes 1048608 | tf_op jit(solution)/shard_map/ppermute | solution.py:216
  155.9 1.5 convert_add_fusion
  157.5 0.1 fusion.3
  157.6 5.9 %collective-permute-start.5 = (bf16[512,512]{1,0:T(8,128)(2,1)S(1)}, bf16[512,512]{1,0:T(8,128)(2,1)S(1)}, u32[]{:S(2)}, u32[]{:S(2)}) collective-permute-start(bf16[512,512]{1,0:T(8,128)(2,1)S(1)} %fusion.3), channel_id=1, source_target_pairs={{0,1},{1,0},{2,3},{3,2},{4,5},{5,4},{6,7},{7,6},{8,9},{9,8},{10,11... | collective-permute-start | bytes 1572872 | tf_op jit(solution)/shard_map/ppermute | solution.py:216
  163.4 3.0 %project.6 = bf16[2,256,512]{2,1,0:T(8,128)(2,1)S(1)} custom-call(s32[1]{0:T(128)} %bitcast.side_ref, bf16[4,256,512]{2,1,0:T(8,128)(2,1)S(1)} %all-to-all-done.3.refs_0_, bf16[2,4,2,512,512]{4,3,2,1,0:T(8,128)(2,1)} %bitcast.36), custom_call_target="tpu_custom_call" | custom-call | tf_op jit(solution)/shard_map/project/pallas_call | solution.py:106
  166.5 0.6 collective-permute-done.3
  167.1 0.1 convert_add_fusion.1
  167.2 0.1 fusion.5
  167.3 6.8 %collective-permute-start.4 = (bf16[256,512]{1,0:T(8,128)(2,1)S(1)}, bf16[256,512]{1,0:T(8,128)(2,1)S(1)}, u32[]{:S(2)}, u32[]{:S(2)}) collective-permute-start(bf16[256,512]{1,0:T(8,128)(2,1)S(1)} %fusion.5), channel_id=1, source_target_pairs={{0,1},{1,0},{2,3},{3,2},{4,5},{5,4},{6,7},{7,6},{8,9},{9,8},{10,11... | collective-permute-start | bytes 786440 | tf_op jit(solution)/shard_map/ppermute | solution.py:216
  174.1 6.5 %collective-permute-done.4 = bf16[256,512]{1,0:T(8,128)(2,1)S(1)} collective-permute-done((bf16[256,512]{1,0:T(8,128)(2,1)S(1)}, bf16[256,512]{1,0:T(8,128)(2,1)S(1)}, u32[]{:S(2)}, u32[]{:S(2)}) %collective-permute-start.4) | collective-permute-done | bytes 262176 | tf_op jit(solution)/shard_map/ppermute | solution.py:216
  180.5 0.1 fusion.4
  180.7 0.0 collective-permute-done.5
  180.7 0.3 fusion.1
  181.0 0.9 pad_maximum_fusion
  (9 shorter events, 0.0 us)
Async XLA Ops:
  6.5 15.4 %copy-start.3 = (bf16[3,768,512]{2,1,0:T(8,128)(2,1)S(1)}, bf16[3,768,512]{2,1,0:T(8,128)(2,1)}, u32[]{:S(2)}) copy-start(bf16[3,768,512]{2,1,0:T(8,128)(2,1)} %param.9) | copy-start | bytes 7077892
  9.4 13.8 %copy-start.5 = (bf16[32,128]{1,0:T(8,128)(2,1)S(1)}, bf16[32,128]{1,0:T(8,128)(2,1)}, u32[]{:S(2)}) copy-start(bf16[32,128]{1,0:T(8,128)(2,1)} %param.12) | copy-start | bytes 24580
  9.4 20.4 %all-to-all-start = ((bf16[16,25,2,512]{3,2,1,0:T(2,128)(2,1)}), bf16[16,25,2,512]{3,2,1,0:T(2,128)(2,1)S(1)}, u32[]{:S(2)}, u32[]{:S(2)}) async-start(bf16[16,25,2,512]{3,2,1,0:T(2,128)(2,1)} %bitcast.37), calls=%async_computation | async-start | bytes 1638400 | tf_op jit(solution)/shard_map/all_to_all | solution.py:161
  16.4 11.0 %copy-start.6 = (s32[16]{0:T(128)S(1)}, s32[16]{0:T(128)}, u32[]{:S(2)}) copy-start(s32[16]{0:T(128)} %param.15) | copy-start | bytes 196
  16.4 11.0 %copy-start.7 = (s32[4]{0:T(128)S(1)}, s32[4]{0:T(128)}, u32[]{:S(2)}) copy-start(s32[4]{0:T(128)} %param.16) | copy-start | bytes 52
  16.4 11.0 %copy-start.8 = (s32[4]{0:T(128)S(1)}, s32[4]{0:T(128)}, u32[]{:S(2)}) copy-start(s32[4]{0:T(128)} %param.17) | copy-start | bytes 52
  16.4 27.8 %collective-permute-start = (bf16[512,512]{1,0:T(8,128)(2,1)}, bf16[512,512]{1,0:T(8,128)(2,1)}, u32[]{:S(2)}, u32[]{:S(2)}) collective-permute-start(bf16[512,512]{1,0:T(8,128)(2,1)} %param.14), channel_id=1, source_target_pairs={{0,0},{1,1},{2,32},{3,33},{4,64},{5,65},{6,96},{7,97},{8,8},{9,9},... | collective-permute-start | bytes 1572872 | tf_op jit(solution)/shard_map/ppermute | solution.py:185
  27.4 10.3 %copy-start.4 = (bf16[7,3,512]{2,0,1:T(8,128)(2,1)S(1)}, bf16[7,3,512]{2,0,1:T(8,128)(2,1)}, u32[]{:S(2)}) copy-start(bf16[7,3,512]{2,0,1:T(8,128)(2,1)} %param.11) | copy-start | bytes 64516
  30.1 9.7 %copy-start = (bf16[4096,256]{1,0:T(8,128)(2,1)S(1)}, bf16[4096,256]{1,0:T(8,128)(2,1)}, u32[]{:S(2)}) copy-start(bf16[4096,256]{1,0:T(8,128)(2,1)} %toeplitz.1.band_ref) | copy-start | bytes 6291460
  30.1 9.7 %copy-start.2 = (f32[512]{0:T(512)S(1)}, f32[512]{0:T(512)}, u32[]{:S(2)}) copy-start(f32[512]{0:T(512)} %param.13) | copy-start | bytes 6148
  31.2 32.1 %all-to-all-start.1 = ((bf16[16,25,512]{2,1,0:T(8,128)(2,1)}), bf16[16,25,512]{2,1,0:T(8,128)(2,1)S(1)}, u32[]{:S(2)}, u32[]{:S(2)}) async-start(bf16[16,25,512]{2,1,0:T(8,128)(2,1)} %copy.15), calls=%async_computation.1 | async-start | bytes 1048576 | tf_op jit(solution)/shard_map/all_to_all | solution.py:161
  37.6 89.0 %all-gather.2.cloned.1.call-start = ((), (), s32[]{:S(2)}) async-start(), calls=%async_computation.4 | async-start | bytes 8912896 | tf_op jit(solution)/shard_map/all_gather | solution.py:197
  37.7 2.1 %copy-start.1 = (bf16[3,512,512]{2,1,0:T(8,128)(2,1)S(1)}, bf16[3,512,512]{2,1,0:T(8,128)(2,1)}, u32[]{:S(2)}) copy-start(bf16[3,512,512]{2,1,0:T(8,128)(2,1)} %slice.32.body_ref) | copy-start | bytes 4718596
  64.8 41.2 %all-to-all-start.2 = ((bf16[4,512,512]{2,1,0:T(8,128)(2,1)}), bf16[4,512,512]{2,1,0:T(8,128)(2,1)}, u32[]{:S(2)}, u32[]{:S(2)}) async-start(bf16[4,512,512]{2,1,0:T(8,128)(2,1)} %broadcast_in_dim.24), calls=%async_computation.2 | async-start | bytes 4194304 | tf_op jit(solution)/shard_map/all_to_all | solution.py:133
  73.3 18.3 %collective-permute-start.1 = (bf16[3,144,512]{2,1,0:T(8,128)(2,1)}, bf16[3,144,512]{2,1,0:T(8,128)(2,1)}, u32[]{:S(2)}, u32[]{:S(2)}) collective-permute-start(bf16[3,144,512]{2,1,0:T(8,128)(2,1)} %get-tuple-element.28), channel_id=1, source_target_pairs={{0,16},{16,32},{32,48},{48,64},{64,80},{80,96},{96,112},{112,128},... | collective-permute-start | bytes 1327112 | tf_op jit(solution)/shard_map/ppermute | solution.py:192
  107.1 37.4 %all-to-all-start.3 = ((bf16[4,256,512]{2,1,0:T(8,128)(2,1)}), bf16[4,256,512]{2,1,0:T(8,128)(2,1)S(1)}, u32[]{:S(2)}, u32[]{:S(2)}) async-start(bf16[4,256,512]{2,1,0:T(8,128)(2,1)} %broadcast_in_dim.25), calls=%async_computation.3 | async-start | bytes 2097152 | tf_op jit(solution)/shard_map/all_to_all | solution.py:133
  131.4 24.5 %collective-permute-start.2 = (bf16[2,512,512]{2,1,0:T(8,128)(2,1)S(1)}, bf16[2,512,512]{2,1,0:T(8,128)(2,1)}, u32[]{:S(2)}, u32[]{:S(2)}) collective-permute-start(bf16[2,512,512]{2,1,0:T(8,128)(2,1)S(1)} %project.5), channel_id=1, source_target_pairs={{0,8},{1,9},{2,10},{3,11},{4,12},{5,13},{6,14},{7,15},{8,0},{9,1},... | collective-permute-start | bytes 3145736 | tf_op jit(solution)/shard_map/ppermute | solution.py:216
  147.5 19.6 %collective-permute-start.3 = (bf16[2,256,512]{2,1,0:T(8,128)(2,1)S(1)}, bf16[2,256,512]{2,1,0:T(8,128)(2,1)S(1)}, u32[]{:S(2)}, u32[]{:S(2)}) collective-permute-start(bf16[2,256,512]{2,1,0:T(8,128)(2,1)S(1)} %project.7), channel_id=1, source_target_pairs={{0,8},{1,9},{2,10},{3,11},{4,12},{5,13},{6,14},{7,15},{8,0},{9,1},... | collective-permute-start | bytes 1572872 | tf_op jit(solution)/shard_map/ppermute | solution.py:216
  157.6 23.1 %collective-permute-start.5 = (bf16[512,512]{1,0:T(8,128)(2,1)S(1)}, bf16[512,512]{1,0:T(8,128)(2,1)S(1)}, u32[]{:S(2)}, u32[]{:S(2)}) collective-permute-start(bf16[512,512]{1,0:T(8,128)(2,1)S(1)} %fusion.3), channel_id=1, source_target_pairs={{0,1},{1,0},{2,3},{3,2},{4,5},{5,4},{6,7},{7,6},{8,9},{9,8},{10,11... | collective-permute-start | bytes 1572872 | tf_op jit(solution)/shard_map/ppermute | solution.py:216
  167.3 13.3 %collective-permute-start.4 = (bf16[256,512]{1,0:T(8,128)(2,1)S(1)}, bf16[256,512]{1,0:T(8,128)(2,1)S(1)}, u32[]{:S(2)}, u32[]{:S(2)}) collective-permute-start(bf16[256,512]{1,0:T(8,128)(2,1)S(1)} %fusion.5), channel_id=1, source_target_pairs={{0,1},{1,0},{2,3},{3,2},{4,5},{5,4},{6,7},{7,6},{8,9},{9,8},{10,11... | collective-permute-start | bytes 786440 | tf_op jit(solution)/shard_map/ppermute | solution.py:216
Sparse Core Ops, SparseCore 0:
  63.5 60.7 all-gather.1

commit v3 on v2

--- a/solution.py
+++ b/solution.py
@@ -99,17 +99,21 @@
         begin += gated_ref.shape[1]
 
 
-def project(runs, weights, side):
+def project(runs, weights, side, dim):
     parts, _, depth = runs[0].shape
     tokens = sum(run.shape[1] for run in runs)
     width = weights.shape[-1]
+
+    def block(s, side):
+        return (side[0], 0, s, 0, 0) if dim == 0 else (s, 0, side[0], 0, 0)
+
     return pl.pallas_call(
         project_kernel,
         grid_spec=pltpu.PrefetchScalarGridSpec(
             num_scalar_prefetch=1,
             grid=(2,),
             in_specs=[pl.BlockSpec(run.shape, lambda s, side: (0, 0, 0)) for run in runs]
-            + [pl.BlockSpec((1, parts, 1, depth, width), lambda s, side: (side[0], 0, s, 0, 0))],
+            + [pl.BlockSpec((1, parts, 1, depth, width), block)],
             out_specs=pl.BlockSpec((1, tokens, width), lambda s, side: (s, 0, 0)),
         ),
         out_shape=jax.ShapeDtypeStruct((2, tokens, width), BF16),
@@ -215,24 +219,24 @@
     def flipped(value, bit):
         return lax.ppermute(value, "chan", [(j, j ^ bit) for j in range(16)])
 
-    def halves(kept, came):
+    def halves(kept, came, place):
         kept = kept.astype(F32) + came.astype(F32)
-        mine = jnp.where(low == 0, kept[0], kept[1])
-        other = jnp.where(low == 0, kept[1], kept[0])
+        mine = jnp.where(place == 0, kept[0], kept[1])
+        other = jnp.where(place == 0, kept[1], kept[0])
         return mine, other.astype(BF16)
 
     def rounded(mine, came):
         return (mine + came.astype(F32)).astype(BF16)
 
-    late_came = flipped(project(late, weights, 1 - high), 8)
-    late_kept = project(late, weights, high)
+    late_came = flipped(project(late, weights, 1 - high, 0), 8)
+    late_kept = project(late, weights, high, 0)
     early, late_kept = lax.optimization_barrier((early, late_kept))
-    early_came = flipped(project(early, weights, 1 - high), 8)
-    late_mine, late_other = halves(late_kept, late_came)
+    early_came = flipped(project(early, weights, 1 - low, 2), 1)
+    late_mine, late_other = halves(late_kept, late_came, low)
     early, late_other = lax.optimization_barrier((early, late_other))
     late_came = flipped(late_other, 1)
-    early_mine, early_other = halves(project(early, weights, high), early_came)
-    early_came = flipped(early_other, 1)
+    early_mine, early_other = halves(project(early, weights, low, 2), early_came, high)
+    early_came = flipped(early_other, 8)
     return jnp.concatenate(
         [rounded(early_mine, early_came), rounded(late_mine, late_came)], axis=0
     )

time: 190 us -> 192 us (1.011)
  no operation moved by 1% of the time
where the time goes in v3:
time: 192 us; the launch traced here: 190 us
  starting transfers between devices  68.3 us (36%)
  waiting for transfers between devices  61.5 us (32%)
  Pallas kernels  26.3 us (14%)
  between operations  14.9 us (8%)
  local copies, waits for them, and re-layouts  13.2 us (7%)
  other arithmetic  5.9 us (3%)
    all_to_all x2, starting transfers between devices, grouped(): lax.all_to_all(value, 'chan', split_axis=0, concat_axis=0, tiled=True, ax...  28 us
    all_to_all x2, waiting for transfers between devices, exchanged(): return lax.all_to_all(value, 'ctx', split_axis=0, concat_axis=0, tiled=True)  21.3 us
    ppermute x4, starting transfers between devices, flipped(): return lax.ppermute(value, 'chan', [(j, j ^ bit) for j in range(16)])  17.5 us
    all_to_all x2, waiting for transfers between devices, grouped(): lax.all_to_all(value, 'chan', split_axis=0, concat_axis=0, tiled=True, ax...  16 us
    pallas_call x4, Pallas kernels, project(): pl.pallas_call(project_kernel, grid_spec=pltpu.PrefetchScalarGridSpec(num...  15.6 us
    ppermute x4, waiting for transfers between devices, flipped(): return lax.ppermute(value, 'chan', [(j, j ^ bit) for j in range(16)])  14.8 us
    all_to_all x2, starting transfers between devices, exchanged(): return lax.all_to_all(value, 'ctx', split_axis=0, concat_axis=0, tiled=True)  13.5 us
    ppermute x1, waiting for transfers between devices, body(): lax.ppermute(features[:, tokens - HEAD:, :], 'ctx', [(i, i + 1) for i in...  9.3 us
  transfers between devices with their start and end apart: 11, of which 8 were waited for; matrix products, arithmetic and copies ran while one was open for 8% of the time, Pallas kernels for 14%

profile of v3, /device:TPU:1, one launch (start us, length us, event | category | flops | bytes accessed | tf_op | source)
XLA Modules:
  0.0 190.5 jit_solution(15109215985258793302)
XLA Ops:
  6.5 2.8 %pad.14 = bf16[400,2,512]{2,1,0:T(2,128)(2,1)} pad(bf16[399,2,512]{2,1,0:T(2,128)(2,1)} %bitcast.41, bf16[]{:T(256)} %constant.20.clone.1), padding=0_1x0_0x0_0 | pad | bytes 1636354 | tf_op jit(solution)/shard_map/jit(_pad)/pad | solution.py:147
  9.4 7.0 %all-to-all-start = ((bf16[16,25,2,512]{3,2,1,0:T(2,128)(2,1)}), bf16[16,25,2,512]{3,2,1,0:T(2,128)(2,1)S(1)}, u32[]{:S(2)}, u32[]{:S(2)}) async-start(bf16[16,25,2,512]{3,2,1,0:T(2,128)(2,1)} %bitcast.39), calls=%async_computation | async-start | bytes 1638400 | tf_op jit(solution)/shard_map/all_to_all | solution.py:165
  16.4 0.0 copy-start.7
  16.4 0.0 copy-start.8
  16.4 5.5 %collective-permute-start = (bf16[512,512]{1,0:T(8,128)(2,1)}, bf16[512,512]{1,0:T(8,128)(2,1)}, u32[]{:S(2)}, u32[]{:S(2)}) collective-permute-start(bf16[512,512]{1,0:T(8,128)(2,1)} %param.14), channel_id=1, source_target_pairs={{0,0},{1,1},{2,32},{3,33},{4,64},{5,65},{6,96},{7,97},{8,8},{9,9},... | collective-permute-start | bytes 1572872 | tf_op jit(solution)/shard_map/ppermute | solution.py:189
  21.9 0.0 copy-done.3
  21.9 1.3 slice.32.body_ref
  23.2 0.0 copy-done.5
  23.2 0.1 rev.3
  23.3 0.7 pad_convert_fusion.rows_ref
  24.0 3.4 %toeplitz.1.band_ref = bf16[4096,256]{1,0:T(8,128)(2,1)} custom-call(f32[32,256]{1,0:T(8,128)} %pad_convert_fusion.rows_ref), custom_call_target="tpu_custom_call" | custom-call | tf_op jit(solution)/shard_map/toeplitz/pallas_call | solution.py:25
  27.4 0.0 copy-done.6
  27.4 0.0 copy-done.7
  27.4 0.0 copy-done.8
  27.4 0.0 copy-start.4
  27.4 0.1 select_reduce_fusion.1
  27.5 0.1 iota_compare_fusion
  27.6 2.2 %all-to-all-done = bf16[16,25,2,512]{3,2,1,0:T(2,128)(2,1)S(1)} async-done(((bf16[16,25,2,512]{3,2,1,0:T(2,128)(2,1)}), bf16[16,25,2,512]{3,2,1,0:T(2,128)(2,1)S(1)}, u32[]{:S(2)}, u32[]{:S(2)}) %all-to-all-start) | async-done | bytes 819232 | tf_op jit(solution)/shard_map/all_to_all | solution.py:165
  29.7 0.4 fusion
  30.1 0.0 copy-start.2
  30.2 1.0 copy.15
  31.2 6.4 %all-to-all-start.1 = ((bf16[16,25,512]{2,1,0:T(8,128)(2,1)}), bf16[16,25,512]{2,1,0:T(8,128)(2,1)S(1)}, u32[]{:S(2)}, u32[]{:S(2)}) async-start(bf16[16,25,512]{2,1,0:T(8,128)(2,1)} %copy.15), calls=%async_computation.1 | async-start | bytes 1048576 | tf_op jit(solution)/shard_map/all_to_all | solution.py:165
  37.6 0.0 all-gather.2.cloned.1.call-start
  37.7 0.0 copy-done.4
  37.7 0.0 copy-start.1
  37.7 2.1 %fusion.12 = (bf16[3,144,512]{2,1,0:T(8,128)(2,1)S(1)}, bf16[3,144,512]{2,1,0:T(8,128)(2,1)}) fusion(bf16[3,768,512]{2,1,0:T(8,128)(2,1)} %param.9), kind=kLoop, calls=%fused_computation.30 | loop fusion | bytes 1769472 | tf_op jit(solution)/shard_map/slice | solution.py:194
  39.8 0.0 copy-done.2
  39.8 4.4 %conv.2 = bf16[512,512]{1,0:T(8,128)(2,1)S(1)} custom-call(bf16[3,144,512]{2,1,0:T(8,128)(2,1)S(1)} %get-tuple-element.27.head_ref, bf16[3,512,512]{2,1,0:T(8,128)(2,1)S(1)} %copy-done.1, f32[3,7,512]{2,1,0:T(8,128)S(1)} %convert_bitcast_fusion.taps_ref, f32[1,512]{1,0:T(1,128)S(1)} %bitcast.33, bf16[4096,256]{1,0:T(8,128)(2,1)S(1)} %copy-done), custom_call_target="tpu_custom_call" | custom-call | tf_op jit(solution)/shard_map/conv/pallas_call | solution.py:69
  44.2 0.0 collective-permute-done
  44.2 19.1 %all-to-all-done.1 = bf16[16,25,512]{2,1,0:T(8,128)(2,1)S(1)} async-done(((bf16[16,25,512]{2,1,0:T(8,128)(2,1)}), bf16[16,25,512]{2,1,0:T(8,128)(2,1)S(1)}, u32[]{:S(2)}, u32[]{:S(2)}) %all-to-all-start.1) | async-done | bytes 409632 | tf_op jit(solution)/shard_map/all_to_all | solution.py:165
  63.3 0.0 all-gather.2.cloned.1.call-update
  63.3 1.5 broadcast_in_dim.24
  64.8 8.5 %all-to-all-start.2 = ((bf16[4,512,512]{2,1,0:T(8,128)(2,1)}), bf16[4,512,512]{2,1,0:T(8,128)(2,1)}, u32[]{:S(2)}, u32[]{:S(2)}) async-start(bf16[4,512,512]{2,1,0:T(8,128)(2,1)} %broadcast_in_dim.24), calls=%async_computation.2 | async-start | bytes 4194304 | tf_op jit(solution)/shard_map/all_to_all | solution.py:137
  73.3 3.7 %collective-permute-start.1 = (bf16[3,144,512]{2,1,0:T(8,128)(2,1)}, bf16[3,144,512]{2,1,0:T(8,128)(2,1)}, u32[]{:S(2)}, u32[]{:S(2)}) collective-permute-start(bf16[3,144,512]{2,1,0:T(8,128)(2,1)} %get-tuple-element.28), channel_id=1, source_target_pairs={{0,16},{16,32},{32,48},{48,64},{64,80},{80,96},{96,112},{112,128},... | collective-permute-start | bytes 1327112 | tf_op jit(solution)/shard_map/ppermute | solution.py:196
  77.0 1.3 slice.35.body_ref
  78.4 0.7 fusion.11
  80.3 0.9 reshape.89
  81.2 1.1 reshape.90
  82.3 9.3 %collective-permute-done.1 = bf16[3,144,512]{2,1,0:T(8,128)(2,1)} collective-permute-done((bf16[3,144,512]{2,1,0:T(8,128)(2,1)}, bf16[3,144,512]{2,1,0:T(8,128)(2,1)}, u32[]{:S(2)}, u32[]{:S(2)}) %collective-permute-start.1) | collective-permute-done | bytes 442400 | tf_op jit(solution)/shard_map/ppermute | solution.py:196
  91.6 1.2 pad_select_fusion.head_ref
  92.8 2.9 %conv.3 = bf16[256,512]{1,0:T(8,128)(2,1)S(1)} custom-call(bf16[3,144,512]{2,1,0:T(8,128)(2,1)S(1)} %pad_select_fusion.head_ref, bf16[3,256,512]{2,1,0:T(8,128)(2,1)S(1)} %slice.35.body_ref, f32[3,7,512]{2,1,0:T(8,128)S(1)} %convert_bitcast_fusion.taps_ref, f32[1,512]{1,0:T(1,128)S(1)} %bitcast.34, bf16[4096,256]{1,0:T(8,128)(2,1)S(1)} %copy-done), custom_call_target="tpu_custom_call" | custom-call | tf_op jit(solution)/shard_map/conv/pallas_call | solution.py:69
  95.7 10.3 %all-to-all-done.2.refs_0_ = bf16[4,512,512]{2,1,0:T(8,128)(2,1)} async-done(((bf16[4,512,512]{2,1,0:T(8,128)(2,1)}), bf16[4,512,512]{2,1,0:T(8,128)(2,1)}, u32[]{:S(2)}, u32[]{:S(2)}) %all-to-all-start.2) | async-done | bytes 2097184 | tf_op jit(solution)/shard_map/all_to_all | solution.py:137
  106.0 1.1 broadcast_in_dim.25
  107.1 19.6 %all-to-all-start.3 = ((bf16[4,256,512]{2,1,0:T(8,128)(2,1)}), bf16[4,256,512]{2,1,0:T(8,128)(2,1)S(1)}, u32[]{:S(2)}, u32[]{:S(2)}) async-start(bf16[4,256,512]{2,1,0:T(8,128)(2,1)} %broadcast_in_dim.25), calls=%async_computation.3 | async-start | bytes 2097152 | tf_op jit(solution)/shard_map/all_to_all | solution.py:137
  126.7 4.7 %project.5 = bf16[2,512,512]{2,1,0:T(8,128)(2,1)S(1)} custom-call(s32[1]{0:T(128)} %bitcast.11.side_ref, bf16[4,512,512]{2,1,0:T(8,128)(2,1)} %all-to-all-done.2.refs_0_, bf16[2,4,2,512,512]{4,3,2,1,0:T(8,128)(2,1)} %bitcast.35), custom_call_target="tpu_custom_call" | custom-call | tf_op jit(solution)/shard_map/project/pallas_call | solution.py:110
  131.4 2.5 %collective-permute-start.2 = (bf16[2,512,512]{2,1,0:T(8,128)(2,1)S(1)}, bf16[2,512,512]{2,1,0:T(8,128)(2,1)}, u32[]{:S(2)}, u32[]{:S(2)}) collective-permute-start(bf16[2,512,512]{2,1,0:T(8,128)(2,1)S(1)} %project.5), channel_id=1, source_target_pairs={{0,8},{1,9},{2,10},{3,11},{4,12},{5,13},{6,14},{7,15},{8,0},{9,1},... | collective-permute-start | bytes 3145736 | tf_op jit(solution)/shard_map/ppermute | solution.py:220
  133.9 4.7 %project.4 = bf16[2,512,512]{2,1,0:T(8,128)(2,1)S(1)} custom-call(s32[1]{0:T(128)} %bitcast.9.side_ref, bf16[4,512,512]{2,1,0:T(8,128)(2,1)} %all-to-all-done.2.refs_0_, bf16[2,4,2,512,512]{4,3,2,1,0:T(8,128)(2,1)} %bitcast.36), custom_call_target="tpu_custom_call" | custom-call | tf_op jit(solution)/shard_map/project/pallas_call | solution.py:110
  138.7 5.8 %all-to-all-done.3.refs_0_ = bf16[4,256,512]{2,1,0:T(8,128)(2,1)S(1)} async-done(((bf16[4,256,512]{2,1,0:T(8,128)(2,1)}), bf16[4,256,512]{2,1,0:T(8,128)(2,1)S(1)}, u32[]{:S(2)}, u32[]{:S(2)}) %all-to-all-start.3) | async-done | bytes 1048608 | tf_op jit(solution)/shard_map/all_to_all | solution.py:137
  144.5 3.0 %project.7 = bf16[2,256,512]{2,1,0:T(8,128)(2,1)S(1)} custom-call(s32[1]{0:T(128)} %bitcast.13.side_ref, bf16[4,256,512]{2,1,0:T(8,128)(2,1)S(1)} %all-to-all-done.3.refs_0_, bf16[2,4,2,512,512]{4,3,2,1,0:T(8,128)(2,1)} %bitcast.37), custom_call_target="tpu_custom_call" | custom-call | tf_op jit(solution)/shard_map/project/pallas_call | solution.py:110
  147.5 11.7 %collective-permute-start.3 = (bf16[2,256,512]{2,1,0:T(8,128)(2,1)S(1)}, bf16[2,256,512]{2,1,0:T(8,128)(2,1)S(1)}, u32[]{:S(2)}, u32[]{:S(2)}) collective-permute-start(bf16[2,256,512]{2,1,0:T(8,128)(2,1)S(1)} %project.7), channel_id=1, source_target_pairs={{0,1},{1,0},{2,3},{3,2},{4,5},{5,4},{6,7},{7,6},{8,9},{9,8},{10,11... | collective-permute-start | bytes 1572872 | tf_op jit(solution)/shard_map/ppermute | solution.py:220
  159.3 0.0 collective-permute-done.2
  159.3 1.5 convert_add_fusion
  160.8 0.1 fusion.3
  160.9 0.7 collective-permute-start.5
  161.6 3.0 %project.6 = bf16[2,256,512]{2,1,0:T(8,128)(2,1)S(1)} custom-call(s32[1]{0:T(128)} %bitcast.side_ref, bf16[4,256,512]{2,1,0:T(8,128)(2,1)S(1)} %all-to-all-done.3.refs_0_, bf16[2,4,2,512,512]{4,3,2,1,0:T(8,128)(2,1)} %bitcast.38), custom_call_target="tpu_custom_call" | custom-call | tf_op jit(solution)/shard_map/project/pallas_call | solution.py:110
  164.6 6.5 %collective-permute-done.3 = bf16[2,256,512]{2,1,0:T(8,128)(2,1)S(1)} collective-permute-done((bf16[2,256,512]{2,1,0:T(8,128)(2,1)S(1)}, bf16[2,256,512]{2,1,0:T(8,128)(2,1)S(1)}, u32[]{:S(2)}, u32[]{:S(2)}) %collective-permute-start.3) | collective-permute-done | bytes 524320 | tf_op jit(solution)/shard_map/ppermute | solution.py:220
  171.1 0.1 convert_add_fusion.1
  171.3 0.1 fusion.5
  171.3 2.5 %collective-permute-start.4 = (bf16[256,512]{1,0:T(8,128)(2,1)S(1)}, bf16[256,512]{1,0:T(8,128)(2,1)S(1)}, u32[]{:S(2)}, u32[]{:S(2)}) collective-permute-start(bf16[256,512]{1,0:T(8,128)(2,1)S(1)} %fusion.5), channel_id=1, source_target_pairs={{0,8},{1,9},{2,10},{3,11},{4,12},{5,13},{6,14},{7,15},{8,0},{9,1},... | collective-permute-start | bytes 786440 | tf_op jit(solution)/shard_map/ppermute | solution.py:220
  173.9 5.2 %collective-permute-done.4 = bf16[256,512]{1,0:T(8,128)(2,1)S(1)} collective-permute-done((bf16[256,512]{1,0:T(8,128)(2,1)S(1)}, bf16[256,512]{1,0:T(8,128)(2,1)S(1)}, u32[]{:S(2)}, u32[]{:S(2)}) %collective-permute-start.4) | collective-permute-done | bytes 262176 | tf_op jit(solution)/shard_map/ppermute | solution.py:220
  179.1 0.1 fusion.4
  179.2 3.1 %collective-permute-done.5 = bf16[512,512]{1,0:T(8,128)(2,1)S(1)} collective-permute-done((bf16[512,512]{1,0:T(8,128)(2,1)S(1)}, bf16[512,512]{1,0:T(8,128)(2,1)S(1)}, u32[]{:S(2)}, u32[]{:S(2)}) %collective-permute-start.5) | collective-permute-done | bytes 524320 | tf_op jit(solution)/shard_map/ppermute | solution.py:220
  182.3 0.3 fusion.1
  182.7 0.9 pad_maximum_fusion
  (9 shorter events, 0.0 us)
Async XLA Ops:
  6.5 15.4 %copy-start.3 = (bf16[3,768,512]{2,1,0:T(8,128)(2,1)S(1)}, bf16[3,768,512]{2,1,0:T(8,128)(2,1)}, u32[]{:S(2)}) copy-start(bf16[3,768,512]{2,1,0:T(8,128)(2,1)} %param.9) | copy-start | bytes 7077892
  9.4 13.8 %copy-start.5 = (bf16[32,128]{1,0:T(8,128)(2,1)S(1)}, bf16[32,128]{1,0:T(8,128)(2,1)}, u32[]{:S(2)}) copy-start(bf16[32,128]{1,0:T(8,128)(2,1)} %param.12) | copy-start | bytes 24580
  9.4 20.4 %all-to-all-start = ((bf16[16,25,2,512]{3,2,1,0:T(2,128)(2,1)}), bf16[16,25,2,512]{3,2,1,0:T(2,128)(2,1)S(1)}, u32[]{:S(2)}, u32[]{:S(2)}) async-start(bf16[16,25,2,512]{3,2,1,0:T(2,128)(2,1)} %bitcast.39), calls=%async_computation | async-start | bytes 1638400 | tf_op jit(solution)/shard_map/all_to_all | solution.py:165
  16.4 11.0 %copy-start.6 = (s32[16]{0:T(128)S(1)}, s32[16]{0:T(128)}, u32[]{:S(2)}) copy-start(s32[16]{0:T(128)} %param.15) | copy-start | bytes 196
  16.4 11.0 %copy-start.7 = (s32[4]{0:T(128)S(1)}, s32[4]{0:T(128)}, u32[]{:S(2)}) copy-start(s32[4]{0:T(128)} %param.16) | copy-start | bytes 52
  16.4 11.0 %copy-start.8 = (s32[4]{0:T(128)S(1)}, s32[4]{0:T(128)}, u32[]{:S(2)}) copy-start(s32[4]{0:T(128)} %param.17) | copy-start | bytes 52
  16.4 27.8 %collective-permute-start = (bf16[512,512]{1,0:T(8,128)(2,1)}, bf16[512,512]{1,0:T(8,128)(2,1)}, u32[]{:S(2)}, u32[]{:S(2)}) collective-permute-start(bf16[512,512]{1,0:T(8,128)(2,1)} %param.14), channel_id=1, source_target_pairs={{0,0},{1,1},{2,32},{3,33},{4,64},{5,65},{6,96},{7,97},{8,8},{9,9},... | collective-permute-start | bytes 1572872 | tf_op jit(solution)/shard_map/ppermute | solution.py:189
  27.4 10.3 %copy-start.4 = (bf16[7,3,512]{2,0,1:T(8,128)(2,1)S(1)}, bf16[7,3,512]{2,0,1:T(8,128)(2,1)}, u32[]{:S(2)}) copy-start(bf16[7,3,512]{2,0,1:T(8,128)(2,1)} %param.11) | copy-start | bytes 64516
  30.1 9.7 %copy-start = (bf16[4096,256]{1,0:T(8,128)(2,1)S(1)}, bf16[4096,256]{1,0:T(8,128)(2,1)}, u32[]{:S(2)}) copy-start(bf16[4096,256]{1,0:T(8,128)(2,1)} %toeplitz.1.band_ref) | copy-start | bytes 6291460
  30.1 9.7 %copy-start.2 = (f32[512]{0:T(512)S(1)}, f32[512]{0:T(512)}, u32[]{:S(2)}) copy-start(f32[512]{0:T(512)} %param.13) | copy-start | bytes 6148
  31.2 32.1 %all-to-all-start.1 = ((bf16[16,25,512]{2,1,0:T(8,128)(2,1)}), bf16[16,25,512]{2,1,0:T(8,128)(2,1)S(1)}, u32[]{:S(2)}, u32[]{:S(2)}) async-start(bf16[16,25,512]{2,1,0:T(8,128)(2,1)} %copy.15), calls=%async_computation.1 | async-start | bytes 1048576 | tf_op jit(solution)/shard_map/all_to_all | solution.py:165
  37.6 89.0 %all-gather.2.cloned.1.call-start = ((), (), s32[]{:S(2)}) async-start(), calls=%async_computation.4 | async-start | bytes 8912896 | tf_op jit(solution)/shard_map/all_gather | solution.py:201
  37.7 2.1 %copy-start.1 = (bf16[3,512,512]{2,1,0:T(8,128)(2,1)S(1)}, bf16[3,512,512]{2,1,0:T(8,128)(2,1)}, u32[]{:S(2)}) copy-start(bf16[3,512,512]{2,1,0:T(8,128)(2,1)} %slice.32.body_ref) | copy-start | bytes 4718596
  64.8 41.2 %all-to-all-start.2 = ((bf16[4,512,512]{2,1,0:T(8,128)(2,1)}), bf16[4,512,512]{2,1,0:T(8,128)(2,1)}, u32[]{:S(2)}, u32[]{:S(2)}) async-start(bf16[4,512,512]{2,1,0:T(8,128)(2,1)} %broadcast_in_dim.24), calls=%async_computation.2 | async-start | bytes 4194304 | tf_op jit(solution)/shard_map/all_to_all | solution.py:137
  73.3 18.3 %collective-permute-start.1 = (bf16[3,144,512]{2,1,0:T(8,128)(2,1)}, bf16[3,144,512]{2,1,0:T(8,128)(2,1)}, u32[]{:S(2)}, u32[]{:S(2)}) collective-permute-start(bf16[3,144,512]{2,1,0:T(8,128)(2,1)} %get-tuple-element.28), channel_id=1, source_target_pairs={{0,16},{16,32},{32,48},{48,64},{64,80},{80,96},{96,112},{112,128},... | collective-permute-start | bytes 1327112 | tf_op jit(solution)/shard_map/ppermute | solution.py:196
  107.1 37.4 %all-to-all-start.3 = ((bf16[4,256,512]{2,1,0:T(8,128)(2,1)}), bf16[4,256,512]{2,1,0:T(8,128)(2,1)S(1)}, u32[]{:S(2)}, u32[]{:S(2)}) async-start(bf16[4,256,512]{2,1,0:T(8,128)(2,1)} %broadcast_in_dim.25), calls=%async_computation.3 | async-start | bytes 2097152 | tf_op jit(solution)/shard_map/all_to_all | solution.py:137
  131.4 27.9 %collective-permute-start.2 = (bf16[2,512,512]{2,1,0:T(8,128)(2,1)S(1)}, bf16[2,512,512]{2,1,0:T(8,128)(2,1)}, u32[]{:S(2)}, u32[]{:S(2)}) collective-permute-start(bf16[2,512,512]{2,1,0:T(8,128)(2,1)S(1)} %project.5), channel_id=1, source_target_pairs={{0,8},{1,9},{2,10},{3,11},{4,12},{5,13},{6,14},{7,15},{8,0},{9,1},... | collective-permute-start | bytes 3145736 | tf_op jit(solution)/shard_map/ppermute | solution.py:220
  147.5 23.6 %collective-permute-start.3 = (bf16[2,256,512]{2,1,0:T(8,128)(2,1)S(1)}, bf16[2,256,512]{2,1,0:T(8,128)(2,1)S(1)}, u32[]{:S(2)}, u32[]{:S(2)}) collective-permute-start(bf16[2,256,512]{2,1,0:T(8,128)(2,1)S(1)} %project.7), channel_id=1, source_target_pairs={{0,1},{1,0},{2,3},{3,2},{4,5},{5,4},{6,7},{7,6},{8,9},{9,8},{10,11... | collective-permute-start | bytes 1572872 | tf_op jit(solution)/shard_map/ppermute | solution.py:220
  160.9 21.5 %collective-permute-start.5 = (bf16[512,512]{1,0:T(8,128)(2,1)S(1)}, bf16[512,512]{1,0:T(8,128)(2,1)S(1)}, u32[]{:S(2)}, u32[]{:S(2)}) collective-permute-start(bf16[512,512]{1,0:T(8,128)(2,1)S(1)} %fusion.3), channel_id=1, source_target_pairs={{0,1},{1,0},{2,3},{3,2},{4,5},{5,4},{6,7},{7,6},{8,9},{9,8},{10,11... | collective-permute-start | bytes 1572872 | tf_op jit(solution)/shard_map/ppermute | solution.py:220
  171.3 7.7 %collective-permute-start.4 = (bf16[256,512]{1,0:T(8,128)(2,1)S(1)}, bf16[256,512]{1,0:T(8,128)(2,1)S(1)}, u32[]{:S(2)}, u32[]{:S(2)}) collective-permute-start(bf16[256,512]{1,0:T(8,128)(2,1)S(1)} %fusion.5), channel_id=1, source_target_pairs={{0,8},{1,9},{2,10},{3,11},{4,12},{5,13},{6,14},{7,15},{8,0},{9,1},... | collective-permute-start | bytes 786440 | tf_op jit(solution)/shard_map/ppermute | solution.py:220
Sparse Core Ops, SparseCore 0:
  63.5 60.7 all-gather.1

commit v4 on v2

--- a/solution.py
+++ b/solution.py
@@ -181,11 +181,12 @@
     def spread(gated):
         return grouped(jnp.broadcast_to(gated, (4, *gated.shape)), rings)
 
-    pieces = exchanged(pool_pieces(pool_tails))
     swapped = lax.ppermute(out_weight, ("ctx", "chan"), swapped_pairs())
     taps = jnp.transpose(short_filter, (1, 0, 2)).astype(F32)
     skip = skip_gain[None, :]
     band = toeplitz(long_filter)
+    pieces, band = lax.optimization_barrier((pool_pieces(pool_tails), band))
+    pieces = exchanged(pieces)
     late = gated_tokens(
         features[:, split - HEAD : split, :], features[:, split:, :], taps, skip, band
     )

time: 190 us -> 193 us (1.016)
  waiting for transfers between devices: 60.6 us -> 64 us
    all_to_all x2, waiting for transfers between devices: 21.3 us -> 25.8 us  [exchanged(): return lax.all_to_all(value, 'ctx', split_axis=0, concat_axis=0, tiled=True)]
  transfers between devices with their start and end apart: 11 -> 11, of which waited for: 8 -> 8; matrix products, arithmetic and copies ran while one was open for 8% -> 8% of each run, Pallas kernels for 14% -> 12%
where the time goes in v4:
time: 193 us; the launch traced here: 192 us
  starting transfers between devices  68 us (35%)
  waiting for transfers between devices  64 us (33%)
  Pallas kernels  26.3 us (14%)
  between operations  14.9 us (8%)
  local copies, waits for them, and re-layouts  12.7 us (7%)
  other arithmetic  5.9 us (3%)
    all_to_all x2, starting transfers between devices, grouped(): lax.all_to_all(value, 'chan', split_axis=0, concat_axis=0, tiled=True, ax...  28.3 us
    all_to_all x2, waiting for transfers between devices, exchanged(): return lax.all_to_all(value, 'ctx', split_axis=0, concat_axis=0, tiled=True)  25.8 us
    ppermute x4, starting transfers between devices, flipped(): return lax.ppermute(value, 'chan', [(j, j ^ bit) for j in range(16)])  17.7 us
    all_to_all x2, waiting for transfers between devices, grouped(): lax.all_to_all(value, 'chan', split_axis=0, concat_axis=0, tiled=True, ax...  16 us
    pallas_call x4, Pallas kernels, project(): pl.pallas_call(project_kernel, grid_spec=pltpu.PrefetchScalarGridSpec(num...  15.6 us
    ppermute x4, waiting for transfers between devices, flipped(): return lax.ppermute(value, 'chan', [(j, j ^ bit) for j in range(16)])  13 us
    all_to_all x2, starting transfers between devices, exchanged(): return lax.all_to_all(value, 'ctx', split_axis=0, concat_axis=0, tiled=True)  12.8 us
    ppermute x1, waiting for transfers between devices, body(): lax.ppermute(features[:, tokens - HEAD:, :], 'ctx', [(i, i + 1) for i in...  9.3 us
  transfers between devices with their start and end apart: 11, of which 8 were waited for; matrix products, arithmetic and copies ran while one was open for 8% of the time, Pallas kernels for 12%

profile of v4, /device:TPU:1, one launch (start us, length us, event | category | flops | bytes accessed | tf_op | source)
XLA Modules:
  0.0 192.2 jit_solution(15912975384432251162)
XLA Ops:
  6.5 0.9 rev.3
  7.4 0.7 pad_convert_fusion.rows_ref
  8.1 3.4 %toeplitz.1.band_ref = bf16[4096,256]{1,0:T(8,128)(2,1)} custom-call(f32[32,256]{1,0:T(8,128)} %pad_convert_fusion.rows_ref), custom_call_target="tpu_custom_call" | custom-call | tf_op jit(solution)/shard_map/toeplitz/pallas_call | solution.py:25
  11.5 0.0 copy-done.4
  11.5 1.5 pad.14
  13.0 7.0 %all-to-all-start = ((bf16[16,25,2,512]{3,2,1,0:T(2,128)(2,1)}), bf16[16,25,2,512]{3,2,1,0:T(2,128)(2,1)S(1)}, u32[]{:S(2)}, u32[]{:S(2)}) async-start(bf16[16,25,2,512]{3,2,1,0:T(2,128)(2,1)} %bitcast.37), calls=%async_computation | async-start | bytes 1638400 | tf_op jit(solution)/shard_map/all_to_all | solution.py:161
  20.1 5.4 %collective-permute-start = (bf16[512,512]{1,0:T(8,128)(2,1)}, bf16[512,512]{1,0:T(8,128)(2,1)}, u32[]{:S(2)}, u32[]{:S(2)}) collective-permute-start(bf16[512,512]{1,0:T(8,128)(2,1)} %param.14), channel_id=1, source_target_pairs={{0,0},{1,1},{2,32},{3,33},{4,64},{5,65},{6,96},{7,97},{8,8},{9,9},... | collective-permute-start | bytes 1572872 | tf_op jit(solution)/shard_map/ppermute | solution.py:184
  25.4 0.0 copy-done.3
  25.4 1.3 slice.32.body_ref
  26.7 0.0 copy-done.6
  26.7 0.0 copy-done.7
  26.7 0.0 copy-done.8
  26.7 0.1 select_reduce_fusion.1
  26.8 0.1 iota_compare_fusion
  26.9 6.5 %all-to-all-done = bf16[16,25,2,512]{3,2,1,0:T(2,128)(2,1)S(1)} async-done(((bf16[16,25,2,512]{3,2,1,0:T(2,128)(2,1)}), bf16[16,25,2,512]{3,2,1,0:T(2,128)(2,1)S(1)}, u32[]{:S(2)}, u32[]{:S(2)}) %all-to-all-start) | async-done | bytes 819232 | tf_op jit(solution)/shard_map/all_to_all | solution.py:161
  33.4 0.4 fusion
  33.8 0.0 copy-start
  33.8 0.0 copy-start.2
  33.8 1.0 copy.15
  34.9 5.7 %all-to-all-start.1 = ((bf16[16,25,512]{2,1,0:T(8,128)(2,1)}), bf16[16,25,512]{2,1,0:T(8,128)(2,1)S(1)}, u32[]{:S(2)}, u32[]{:S(2)}) async-start(bf16[16,25,512]{2,1,0:T(8,128)(2,1)} %copy.15), calls=%async_computation.1 | async-start | bytes 1048576 | tf_op jit(solution)/shard_map/all_to_all | solution.py:161
  40.6 0.0 all-gather.2.cloned.1.call-start
  40.6 0.0 copy-done.5
  40.7 0.0 copy-start.1
  40.7 2.1 %fusion.12 = (bf16[3,144,512]{2,1,0:T(8,128)(2,1)S(1)}, bf16[3,144,512]{2,1,0:T(8,128)(2,1)}) fusion(bf16[3,768,512]{2,1,0:T(8,128)(2,1)} %param.9), kind=kLoop, calls=%fused_computation.30 | loop fusion | bytes 1769472 | tf_op jit(solution)/shard_map/slice | solution.py:191
  42.8 0.0 copy-done
  42.8 0.0 copy-done.2
  42.8 0.0 copy-done.1
  42.8 4.4 %conv.2 = bf16[512,512]{1,0:T(8,128)(2,1)S(1)} custom-call(bf16[3,144,512]{2,1,0:T(8,128)(2,1)S(1)} %get-tuple-element.31.head_ref, bf16[3,512,512]{2,1,0:T(8,128)(2,1)S(1)} %copy-done.1, f32[3,7,512]{2,1,0:T(8,128)S(1)} %convert_bitcast_fusion.taps_ref, f32[1,512]{1,0:T(1,128)S(1)} %bitcast.31, bf16[4096,256]{1,0:T(8,128)(2,1)S(1)} %copy-done), custom_call_target="tpu_custom_call" | custom-call | tf_op jit(solution)/shard_map/conv/pallas_call | solution.py:69
  47.2 0.0 collective-permute-done
  47.2 19.2 %all-to-all-done.1 = bf16[16,25,512]{2,1,0:T(8,128)(2,1)S(1)} async-done(((bf16[16,25,512]{2,1,0:T(8,128)(2,1)}), bf16[16,25,512]{2,1,0:T(8,128)(2,1)S(1)}, u32[]{:S(2)}, u32[]{:S(2)}) %all-to-all-start.1) | async-done | bytes 409632 | tf_op jit(solution)/shard_map/all_to_all | solution.py:161
  66.4 0.0 all-gather.2.cloned.1.call-update
  66.4 1.5 broadcast_in_dim.24
  67.9 8.8 %all-to-all-start.2 = ((bf16[4,512,512]{2,1,0:T(8,128)(2,1)}), bf16[4,512,512]{2,1,0:T(8,128)(2,1)}, u32[]{:S(2)}, u32[]{:S(2)}) async-start(bf16[4,512,512]{2,1,0:T(8,128)(2,1)} %broadcast_in_dim.24), calls=%async_computation.2 | async-start | bytes 4194304 | tf_op jit(solution)/shard_map/all_to_all | solution.py:133
  76.7 3.8 %collective-permute-start.1 = (bf16[3,144,512]{2,1,0:T(8,128)(2,1)}, bf16[3,144,512]{2,1,0:T(8,128)(2,1)}, u32[]{:S(2)}, u32[]{:S(2)}) collective-permute-start(bf16[3,144,512]{2,1,0:T(8,128)(2,1)} %get-tuple-element.32), channel_id=1, source_target_pairs={{0,16},{16,32},{32,48},{48,64},{64,80},{80,96},{96,112},{112,128},... | collective-permute-start | bytes 1327112 | tf_op jit(solution)/shard_map/ppermute | solution.py:193
  80.5 1.3 slice.35.body_ref
  81.9 0.7 fusion.11
  83.8 0.9 reshape.85
  84.7 1.1 reshape.86
  85.8 9.3 %collective-permute-done.1 = bf16[3,144,512]{2,1,0:T(8,128)(2,1)} collective-permute-done((bf16[3,144,512]{2,1,0:T(8,128)(2,1)}, bf16[3,144,512]{2,1,0:T(8,128)(2,1)}, u32[]{:S(2)}, u32[]{:S(2)}) %collective-permute-start.1) | collective-permute-done | bytes 442400 | tf_op jit(solution)/shard_map/ppermute | solution.py:193
  95.1 1.2 pad_select_fusion.head_ref
  96.3 2.9 %conv.3 = bf16[256,512]{1,0:T(8,128)(2,1)S(1)} custom-call(bf16[3,144,512]{2,1,0:T(8,128)(2,1)S(1)} %pad_select_fusion.head_ref, bf16[3,256,512]{2,1,0:T(8,128)(2,1)S(1)} %slice.35.body_ref, f32[3,7,512]{2,1,0:T(8,128)S(1)} %convert_bitcast_fusion.taps_ref, f32[1,512]{1,0:T(1,128)S(1)} %bitcast.32, bf16[4096,256]{1,0:T(8,128)(2,1)S(1)} %copy-done), custom_call_target="tpu_custom_call" | custom-call | tf_op jit(solution)/shard_map/conv/pallas_call | solution.py:69
  99.2 10.2 %all-to-all-done.2.refs_0_ = bf16[4,512,512]{2,1,0:T(8,128)(2,1)} async-done(((bf16[4,512,512]{2,1,0:T(8,128)(2,1)}), bf16[4,512,512]{2,1,0:T(8,128)(2,1)}, u32[]{:S(2)}, u32[]{:S(2)}) %all-to-all-start.2) | async-done | bytes 2097184 | tf_op jit(solution)/shard_map/all_to_all | solution.py:133
  109.4 1.1 broadcast_in_dim.25
  110.5 19.5 %all-to-all-start.3 = ((bf16[4,256,512]{2,1,0:T(8,128)(2,1)}), bf16[4,256,512]{2,1,0:T(8,128)(2,1)S(1)}, u32[]{:S(2)}, u32[]{:S(2)}) async-start(bf16[4,256,512]{2,1,0:T(8,128)(2,1)} %broadcast_in_dim.25), calls=%async_computation.3 | async-start | bytes 2097152 | tf_op jit(solution)/shard_map/all_to_all | solution.py:133
  130.0 4.7 %project.5 = bf16[2,512,512]{2,1,0:T(8,128)(2,1)S(1)} custom-call(s32[1]{0:T(128)} %bitcast.10.side_ref, bf16[4,512,512]{2,1,0:T(8,128)(2,1)} %all-to-all-done.2.refs_0_, bf16[2,4,2,512,512]{4,3,2,1,0:T(8,128)(2,1)} %bitcast.33), custom_call_target="tpu_custom_call" | custom-call | tf_op jit(solution)/shard_map/project/pallas_call | solution.py:106
  134.8 2.5 %collective-permute-start.2 = (bf16[2,512,512]{2,1,0:T(8,128)(2,1)S(1)}, bf16[2,512,512]{2,1,0:T(8,128)(2,1)}, u32[]{:S(2)}, u32[]{:S(2)}) collective-permute-start(bf16[2,512,512]{2,1,0:T(8,128)(2,1)S(1)} %project.5), channel_id=1, source_target_pairs={{0,8},{1,9},{2,10},{3,11},{4,12},{5,13},{6,14},{7,15},{8,0},{9,1},... | collective-permute-start | bytes 3145736 | tf_op jit(solution)/shard_map/ppermute | solution.py:217
  137.3 4.7 %project.4 = bf16[2,512,512]{2,1,0:T(8,128)(2,1)S(1)} custom-call(s32[1]{0:T(128)} %bitcast.side_ref, bf16[4,512,512]{2,1,0:T(8,128)(2,1)} %all-to-all-done.2.refs_0_, bf16[2,4,2,512,512]{4,3,2,1,0:T(8,128)(2,1)} %bitcast.34), custom_call_target="tpu_custom_call" | custom-call | tf_op jit(solution)/shard_map/project/pallas_call | solution.py:106
  142.1 5.7 %all-to-all-done.3.refs_0_ = bf16[4,256,512]{2,1,0:T(8,128)(2,1)S(1)} async-done(((bf16[4,256,512]{2,1,0:T(8,128)(2,1)}), bf16[4,256,512]{2,1,0:T(8,128)(2,1)S(1)}, u32[]{:S(2)}, u32[]{:S(2)}) %all-to-all-start.3) | async-done | bytes 1048608 | tf_op jit(solution)/shard_map/all_to_all | solution.py:133
  147.8 3.0 %project.7 = bf16[2,256,512]{2,1,0:T(8,128)(2,1)S(1)} custom-call(s32[1]{0:T(128)} %bitcast.10.side_ref, bf16[4,256,512]{2,1,0:T(8,128)(2,1)S(1)} %all-to-all-done.3.refs_0_, bf16[2,4,2,512,512]{4,3,2,1,0:T(8,128)(2,1)} %bitcast.35), custom_call_target="tpu_custom_call" | custom-call | tf_op jit(solution)/shard_map/project/pallas_call | solution.py:106
  150.9 2.5 %collective-permute-start.3 = (bf16[2,256,512]{2,1,0:T(8,128)(2,1)S(1)}, bf16[2,256,512]{2,1,0:T(8,128)(2,1)S(1)}, u32[]{:S(2)}, u32[]{:S(2)}) collective-permute-start(bf16[2,256,512]{2,1,0:T(8,128)(2,1)S(1)} %project.7), channel_id=1, source_target_pairs={{0,8},{1,9},{2,10},{3,11},{4,12},{5,13},{6,14},{7,15},{8,0},{9,1},... | collective-permute-start | bytes 1572872 | tf_op jit(solution)/shard_map/ppermute | solution.py:217
  153.4 5.9 %collective-permute-done.2 = bf16[2,512,512]{2,1,0:T(8,128)(2,1)} collective-permute-done((bf16[2,512,512]{2,1,0:T(8,128)(2,1)S(1)}, bf16[2,512,512]{2,1,0:T(8,128)(2,1)}, u32[]{:S(2)}, u32[]{:S(2)}) %collective-permute-start.2) | collective-permute-done | bytes 1048608 | tf_op jit(solution)/shard_map/ppermute | solution.py:217
  159.3 1.5 convert_add_fusion
  160.8 0.1 fusion.3
  160.9 5.9 %collective-permute-start.5 = (bf16[512,512]{1,0:T(8,128)(2,1)S(1)}, bf16[512,512]{1,0:T(8,128)(2,1)S(1)}, u32[]{:S(2)}, u32[]{:S(2)}) collective-permute-start(bf16[512,512]{1,0:T(8,128)(2,1)S(1)} %fusion.3), channel_id=1, source_target_pairs={{0,1},{1,0},{2,3},{3,2},{4,5},{5,4},{6,7},{7,6},{8,9},{9,8},{10,11... | collective-permute-start | bytes 1572872 | tf_op jit(solution)/shard_map/ppermute | solution.py:217
  166.8 3.0 %project.6 = bf16[2,256,512]{2,1,0:T(8,128)(2,1)S(1)} custom-call(s32[1]{0:T(128)} %bitcast.side_ref, bf16[4,256,512]{2,1,0:T(8,128)(2,1)S(1)} %all-to-all-done.3.refs_0_, bf16[2,4,2,512,512]{4,3,2,1,0:T(8,128)(2,1)} %bitcast.36), custom_call_target="tpu_custom_call" | custom-call | tf_op jit(solution)/shard_map/project/pallas_call | solution.py:106
  169.9 0.6 collective-permute-done.3
  170.4 0.1 convert_add_fusion.1
  170.6 0.1 fusion.5
  170.6 6.8 %collective-permute-start.4 = (bf16[256,512]{1,0:T(8,128)(2,1)S(1)}, bf16[256,512]{1,0:T(8,128)(2,1)S(1)}, u32[]{:S(2)}, u32[]{:S(2)}) collective-permute-start(bf16[256,512]{1,0:T(8,128)(2,1)S(1)} %fusion.5), channel_id=1, source_target_pairs={{0,1},{1,0},{2,3},{3,2},{4,5},{5,4},{6,7},{7,6},{8,9},{9,8},{10,11... | collective-permute-start | bytes 786440 | tf_op jit(solution)/shard_map/ppermute | solution.py:217
  177.4 6.5 %collective-permute-done.4 = bf16[256,512]{1,0:T(8,128)(2,1)S(1)} collective-permute-done((bf16[256,512]{1,0:T(8,128)(2,1)S(1)}, bf16[256,512]{1,0:T(8,128)(2,1)S(1)}, u32[]{:S(2)}, u32[]{:S(2)}) %collective-permute-start.4) | collective-permute-done | bytes 262176 | tf_op jit(solution)/shard_map/ppermute | solution.py:217
  183.9 0.1 fusion.4
  184.1 0.0 collective-permute-done.5
  184.1 0.3 fusion.1
  184.4 0.9 pad_maximum_fusion
  (9 shorter events, 0.0 us)
Async XLA Ops:
  6.5 5.0 %copy-start.4 = (bf16[2,3,133,512]{3,0,2,1:T(2,128)(2,1)S(1)}, bf16[2,3,133,512]{3,0,2,1:T(2,128)(2,1)}, u32[]{:S(2)}) copy-start(bf16[2,3,133,512]{3,0,2,1:T(2,128)(2,1)} %param.10) | copy-start | bytes 2451460
  11.5 13.9 %copy-start.3 = (bf16[3,768,512]{2,1,0:T(8,128)(2,1)S(1)}, bf16[3,768,512]{2,1,0:T(8,128)(2,1)}, u32[]{:S(2)}) copy-start(bf16[3,768,512]{2,1,0:T(8,128)(2,1)} %param.9) | copy-start | bytes 7077892
  13.0 13.7 %copy-start.6 = (s32[16]{0:T(128)S(1)}, s32[16]{0:T(128)}, u32[]{:S(2)}) copy-start(s32[16]{0:T(128)} %param.15) | copy-start | bytes 196
  13.0 13.7 %copy-start.7 = (s32[4]{0:T(128)S(1)}, s32[4]{0:T(128)}, u32[]{:S(2)}) copy-start(s32[4]{0:T(128)} %param.16) | copy-start | bytes 52
  13.0 13.7 %copy-start.8 = (s32[4]{0:T(128)S(1)}, s32[4]{0:T(128)}, u32[]{:S(2)}) copy-start(s32[4]{0:T(128)} %param.17) | copy-start | bytes 52
  13.0 20.4 %all-to-all-start = ((bf16[16,25,2,512]{3,2,1,0:T(2,128)(2,1)}), bf16[16,25,2,512]{3,2,1,0:T(2,128)(2,1)S(1)}, u32[]{:S(2)}, u32[]{:S(2)}) async-start(bf16[16,25,2,512]{3,2,1,0:T(2,128)(2,1)} %bitcast.37), calls=%async_computation | async-start | bytes 1638400 | tf_op jit(solution)/shard_map/all_to_all | solution.py:161
  20.1 27.1 %collective-permute-start = (bf16[512,512]{1,0:T(8,128)(2,1)}, bf16[512,512]{1,0:T(8,128)(2,1)}, u32[]{:S(2)}, u32[]{:S(2)}) collective-permute-start(bf16[512,512]{1,0:T(8,128)(2,1)} %param.14), channel_id=1, source_target_pairs={{0,0},{1,1},{2,32},{3,33},{4,64},{5,65},{6,96},{7,97},{8,8},{9,9},... | collective-permute-start | bytes 1572872 | tf_op jit(solution)/shard_map/ppermute | solution.py:184
  26.7 13.9 %copy-start.5 = (bf16[7,3,512]{2,0,1:T(8,128)(2,1)S(1)}, bf16[7,3,512]{2,0,1:T(8,128)(2,1)}, u32[]{:S(2)}) copy-start(bf16[7,3,512]{2,0,1:T(8,128)(2,1)} %param.11) | copy-start | bytes 64516
  33.8 9.0 %copy-start = (bf16[4096,256]{1,0:T(8,128)(2,1)S(1)}, bf16[4096,256]{1,0:T(8,128)(2,1)}, u32[]{:S(2)}) copy-start(bf16[4096,256]{1,0:T(8,128)(2,1)} %toeplitz.1.band_ref) | copy-start | bytes 6291460
  33.8 9.0 %copy-start.2 = (f32[512]{0:T(512)S(1)}, f32[512]{0:T(512)}, u32[]{:S(2)}) copy-start(f32[512]{0:T(512)} %param.13) | copy-start | bytes 6148
  34.9 31.6 %all-to-all-start.1 = ((bf16[16,25,512]{2,1,0:T(8,128)(2,1)}), bf16[16,25,512]{2,1,0:T(8,128)(2,1)S(1)}, u32[]{:S(2)}, u32[]{:S(2)}) async-start(bf16[16,25,512]{2,1,0:T(8,128)(2,1)} %copy.15), calls=%async_computation.1 | async-start | bytes 1048576 | tf_op jit(solution)/shard_map/all_to_all | solution.py:161
  40.6 89.4 %all-gather.2.cloned.1.call-start = ((), (), s32[]{:S(2)}) async-start(), calls=%async_computation.4 | async-start | bytes 8912896 | tf_op jit(solution)/shard_map/all_gather | solution.py:198
  40.7 2.1 %copy-start.1 = (bf16[3,512,512]{2,1,0:T(8,128)(2,1)S(1)}, bf16[3,512,512]{2,1,0:T(8,128)(2,1)}, u32[]{:S(2)}) copy-start(bf16[3,512,512]{2,1,0:T(8,128)(2,1)} %slice.32.body_ref) | copy-start | bytes 4718596
  67.9 41.5 %all-to-all-start.2 = ((bf16[4,512,512]{2,1,0:T(8,128)(2,1)}), bf16[4,512,512]{2,1,0:T(8,128)(2,1)}, u32[]{:S(2)}, u32[]{:S(2)}) async-start(bf16[4,512,512]{2,1,0:T(8,128)(2,1)} %broadcast_in_dim.24), calls=%async_computation.2 | async-start | bytes 4194304 | tf_op jit(solution)/shard_map/all_to_all | solution.py:133
  76.7 18.4 %collective-permute-start.1 = (bf16[3,144,512]{2,1,0:T(8,128)(2,1)}, bf16[3,144,512]{2,1,0:T(8,128)(2,1)}, u32[]{:S(2)}, u32[]{:S(2)}) collective-permute-start(bf16[3,144,512]{2,1,0:T(8,128)(2,1)} %get-tuple-element.32), channel_id=1, source_target_pairs={{0,16},{16,32},{32,48},{48,64},{64,80},{80,96},{96,112},{112,128},... | collective-permute-start | bytes 1327112 | tf_op jit(solution)/shard_map/ppermute | solution.py:193
  110.5 37.3 %all-to-all-start.3 = ((bf16[4,256,512]{2,1,0:T(8,128)(2,1)}), bf16[4,256,512]{2,1,0:T(8,128)(2,1)S(1)}, u32[]{:S(2)}, u32[]{:S(2)}) async-start(bf16[4,256,512]{2,1,0:T(8,128)(2,1)} %broadcast_in_dim.25), calls=%async_computation.3 | async-start | bytes 2097152 | tf_op jit(solution)/shard_map/all_to_all | solution.py:133
  134.8 24.5 %collective-permute-start.2 = (bf16[2,512,512]{2,1,0:T(8,128)(2,1)S(1)}, bf16[2,512,512]{2,1,0:T(8,128)(2,1)}, u32[]{:S(2)}, u32[]{:S(2)}) collective-permute-start(bf16[2,512,512]{2,1,0:T(8,128)(2,1)S(1)} %project.5), channel_id=1, source_target_pairs={{0,8},{1,9},{2,10},{3,11},{4,12},{5,13},{6,14},{7,15},{8,0},{9,1},... | collective-permute-start | bytes 3145736 | tf_op jit(solution)/shard_map/ppermute | solution.py:217
  150.9 19.6 %collective-permute-start.3 = (bf16[2,256,512]{2,1,0:T(8,128)(2,1)S(1)}, bf16[2,256,512]{2,1,0:T(8,128)(2,1)S(1)}, u32[]{:S(2)}, u32[]{:S(2)}) collective-permute-start(bf16[2,256,512]{2,1,0:T(8,128)(2,1)S(1)} %project.7), channel_id=1, source_target_pairs={{0,8},{1,9},{2,10},{3,11},{4,12},{5,13},{6,14},{7,15},{8,0},{9,1},... | collective-permute-start | bytes 1572872 | tf_op jit(solution)/shard_map/ppermute | solution.py:217
  160.9 23.1 %collective-permute-start.5 = (bf16[512,512]{1,0:T(8,128)(2,1)S(1)}, bf16[512,512]{1,0:T(8,128)(2,1)S(1)}, u32[]{:S(2)}, u32[]{:S(2)}) collective-permute-start(bf16[512,512]{1,0:T(8,128)(2,1)S(1)} %fusion.3), channel_id=1, source_target_pairs={{0,1},{1,0},{2,3},{3,2},{4,5},{5,4},{6,7},{7,6},{8,9},{9,8},{10,11... | collective-permute-start | bytes 1572872 | tf_op jit(solution)/shard_map/ppermute | solution.py:217
  170.6 13.3 %collective-permute-start.4 = (bf16[256,512]{1,0:T(8,128)(2,1)S(1)}, bf16[256,512]{1,0:T(8,128)(2,1)S(1)}, u32[]{:S(2)}, u32[]{:S(2)}) collective-permute-start(bf16[256,512]{1,0:T(8,128)(2,1)S(1)} %fusion.5), channel_id=1, source_target_pairs={{0,1},{1,0},{2,3},{3,2},{4,5},{5,4},{6,7},{7,6},{8,9},{9,8},{10,11... | collective-permute-start | bytes 786440 | tf_op jit(solution)/shard_map/ppermute | solution.py:217
Sparse Core Ops, SparseCore 0:
  66.6 61.1 all-gather.1
